TPU v7x, 128 devices: a whole 4x4x4 slice. The times are simulated.
128 devices in a mesh: sx: 16 (over z, x), sy: 8 (over y, core).
Axes of the slice: x: 4, y: 4, z: 4, core: 2. Of those that a mesh axis runs over, the one named last changes fastest.
Arguments:
- activations: bfloat16 [65536, 1024], P(('sx', 'sy')), may hold values from -6 to 6
- norm_gain: float32 [1024], replicated, may hold values from 0.5 to 8
- w_local: bfloat16 [1024, 1536], replicated, may hold values from -0.1875 to 0.1875
- w_cluster: bfloat16 [1024, 3072], replicated, may hold values from -0.1875 to 0.1875
- w_output: bfloat16 [1536, 1024], replicated, may hold values from -0.15625 to 0.15625
- assignment: int32 [65536, 8], P(('sx', 'sy')), may hold values from 0 to 31, as said below
Outputs:
- layer_out: bfloat16 [65536, 1024], P(('sx', 'sy'))
Inputs may be any that keep to these rules, and one draw needn't show every extreme that they name: `assignment`: tokens d * 512 to (d + 1) * 512 - 1 form block d. In every head each cluster number is given to exactly 2048 tokens; at most 28 tokens of one block share a cluster number in one head, and in every head some block has exactly 28. Task group g of head h is the clusters g * 2 to (g + 1) * 2 - 1; at most 40 tokens of one block fall into one task group of one head, and in every head some block has exactly 40 in some group.
All inputs are finite; a program needn't handle non-finite values.
Results may differ from a plain program's by a relative error of at most 0.0035.
The roundings to bfloat16 on the way count: a program that leaves them out, or rounds other values in their place, can miss the bound.
Values may be sent and summed in bfloat16 or wider, within the bound.
No kernel may reach another device: no remote copies, remote signals or barrier semaphores. Data moves between devices by JAX's collectives and lax.ppermute only.
A program may use at most 128 MiB of HBM per device.

v0:
```python
import jax
import jax.numpy as jnp
from jax import lax
from jax.sharding import PartitionSpec as P

HL = 4
HC = 8
HD = 128
WIN = 512
CSIZE = 2048


EPSILON = 1e-06


def shifted(value, axis, steps):
    count = lax.axis_size(axis)
    leading, last = (max(0, -steps), min(count, count - steps))
    return lax.ppermute(value, axis, [(source, source + steps) for source in range(leading, last)])


def rms_norm(activations, norm_gain):
    values = activations.astype(jnp.float32)
    mean_square = jnp.mean(values * values, axis=-1, keepdims=True)
    return (values * lax.rsqrt(mean_square + EPSILON) * norm_gain).astype(jnp.bfloat16)


def normalize_rows(scores):
    highest = jnp.max(scores, axis=-1, keepdims=True)
    raised = jnp.exp(scores - highest)
    return (raised / jnp.sum(raised, axis=-1, keepdims=True)).astype(jnp.bfloat16)


def window_attention(local_qkv, rim_rows, base_row, tok_rows):
    head_width = HL * HD
    score_scale = HD ** (-0.5)
    queries = local_qkv[:, :head_width]
    key_value = jnp.concatenate([rim_rows, local_qkv[:, head_width:]], axis=0)
    block_rows = min(512, tok_rows)

    def window_one_block(first_row):
        query_block = queries.reshape(block_rows, HL, HD)
        key_block = key_value[:, :head_width].reshape(block_rows + WIN, HL, HD)
        value_block = key_value[:, head_width:].reshape(block_rows + WIN, HL, HD)
        scores = (
            jnp.einsum("qhd,khd->hqk", query_block, key_block, preferred_element_type=jnp.float32)
            * score_scale
        )
        row_ids = jnp.arange(block_rows, dtype=jnp.int32)[:, None]
        col_ids = jnp.arange(block_rows + WIN, dtype=jnp.int32)[None, :]
        allowed = (
            (col_ids > row_ids)
            & (col_ids <= row_ids + WIN)
            & (base_row + first_row + col_ids - WIN >= 0)
        )
        scores = jnp.where(allowed[None], scores, -1e30)
        weights = normalize_rows(scores)
        mixed = jnp.einsum("hqk,khd->qhd", weights, value_block, preferred_element_type=jnp.float32)
        return mixed.astype(jnp.bfloat16).reshape(block_rows, head_width)

    starts = jnp.arange(tok_rows // block_rows, dtype=jnp.int32) * block_rows
    return lax.map(window_one_block, starts).reshape(tok_rows, head_width)


def tagged_attention(rows, query_tags, key_tags):
    score_scale = HD ** (-0.5)
    total = rows.shape[0]
    block_rows = total
    while block_rows > 512 and block_rows % 2 == 0:
        block_rows = block_rows // 2
    queries = rows[:, :HD]
    key_rows = rows[:, HD : 2 * HD]
    value_rows = rows[:, 2 * HD :]

    def tagged_one_block(first_row):
        query_block = lax.dynamic_slice_in_dim(queries, first_row, block_rows, 0)
        tag_block = lax.dynamic_slice_in_dim(query_tags, first_row, block_rows, 0)
        scores = (
            jnp.einsum("qd,kd->qk", query_block, key_rows, preferred_element_type=jnp.float32)
            * score_scale
        )
        scores = jnp.where(tag_block[:, None] == key_tags[None, :], scores, -1e30)
        weights = normalize_rows(scores)
        return jnp.dot(weights, value_rows, preferred_element_type=jnp.float32).astype(jnp.bfloat16)

    starts = jnp.arange(total // block_rows, dtype=jnp.int32) * block_rows
    return lax.map(tagged_one_block, starts).reshape(total, HD)


def pooled_tasks(pool_rows, pool_counts):
    sources, pool_size = (pool_rows.shape[0], pool_rows.shape[1])
    task_slots = pool_counts.shape[1]
    bounds = jnp.cumsum(pool_counts, axis=1)
    slot_ids = jnp.arange(pool_size, dtype=jnp.int32)
    task_of = jnp.sum(
        (bounds[:, None, :] <= slot_ids[None, :, None]).astype(jnp.int32), axis=2
    ).reshape(-1)
    alive = task_of < task_slots
    key_tags = jnp.where(alive, task_of, -1)
    result = tagged_attention(pool_rows.reshape(-1, 3 * HD), task_of, key_tags)
    result = jnp.where(alive[:, None], result, jnp.zeros_like(result))
    return result.reshape(sources, pool_size, HD)


def route_plan(assignment, cluster_count):
    tok_rows = assignment.shape[0]
    member = assignment[:, :, None] == jnp.arange(cluster_count, dtype=jnp.int32)[None, None, :]
    onehot = member.astype(jnp.bfloat16).reshape(tok_rows, HC * cluster_count)
    row_ids = jnp.arange(tok_rows, dtype=jnp.int32)
    earlier = (row_ids[:, None] > row_ids[None, :]).astype(jnp.bfloat16)
    running = jnp.dot(earlier, onehot, preferred_element_type=jnp.float32).reshape(
        tok_rows, HC, cluster_count
    )
    member_int = member.astype(jnp.int32)
    position = jnp.sum(jnp.where(member, running, 0.0), axis=2).astype(jnp.int32)
    per_task = jnp.sum(member_int, axis=0).reshape(-1)
    return (member_int, position, per_task)


def place_rows(slot_local, region, qkv_heads):
    slot_ids = jnp.arange(region, dtype=jnp.int32)
    table = (slot_ids[None, :, None] == jnp.transpose(slot_local)[:, None, :]).astype(jnp.bfloat16)
    placed = jnp.einsum(
        "hst,thf->hsf", table, qkv_heads, preferred_element_type=jnp.float32
    ).astype(jnp.bfloat16)
    return (table, placed)


def collect_rows(table, came_back, region):
    heads_back = came_back.reshape(HC, region, HD)
    mixed = jnp.einsum(
        "hst,hsf->thf", table, heads_back, preferred_element_type=jnp.float32
    ).astype(jnp.bfloat16)
    return mixed.reshape(mixed.shape[0], HC * HD)


def body(activations, norm_gain, w_local, w_cluster, w_output, assignment):
    tok_rows = activations.shape[0]
    shards = lax.axis_size(("sx", "sy"))
    mean_rows = CSIZE // shards
    task_slots = tok_rows * HC // CSIZE
    pool_size = (
        task_slots * mean_rows + mean_rows // 2 * (task_slots % 2) + task_slots * (mean_rows // 4)
    )
    cluster_count = shards * task_slots // HC
    head_width = HL * HD
    normed = rms_norm(activations, norm_gain)
    local_qkv = jnp.dot(normed, w_local, preferred_element_type=jnp.float32).astype(jnp.bfloat16)
    cluster_qkv = jnp.dot(normed, w_cluster, preferred_element_type=jnp.float32).astype(
        jnp.bfloat16
    )
    member_int, position, per_task = route_plan(assignment, cluster_count)
    send_counts = per_task.reshape(shards, task_slots)
    qkv_heads = cluster_qkv.reshape(tok_rows, HC, 3 * HD)
    rim_rows = shifted(local_qkv[tok_rows - WIN :, head_width:], ("sx", "sy"), 1)
    base_row = lax.axis_index(("sx", "sy")) * tok_rows
    local_mix = window_attention(local_qkv, rim_rows, base_row, tok_rows)
    offsets = (jnp.cumsum(send_counts, axis=1) - send_counts).reshape(HC, cluster_count)
    offset_of = jnp.sum(member_int * offsets[None, :, :], axis=2)
    groups_head = cluster_count // task_slots
    region = groups_head * pool_size
    local_group = assignment // task_slots
    slot_local = local_group * pool_size + offset_of + position
    table, placed = place_rows(slot_local, region, qkv_heads)
    send_pool = placed.reshape(shards, pool_size, 3 * HD)
    got_pool, got_counts = (
        lax.all_to_all(send_pool, ("sx", "sy"), split_axis=0, concat_axis=0, tiled=True),
        lax.all_to_all(send_counts, ("sx", "sy"), split_axis=0, concat_axis=0, tiled=True),
    )
    finished = pooled_tasks(got_pool, got_counts)
    came_back = lax.all_to_all(finished, ("sx", "sy"), split_axis=0, concat_axis=0, tiled=True)
    cluster_mix = collect_rows(table, came_back, region)
    combined = jnp.concatenate([local_mix, cluster_mix], axis=1)
    projected = jnp.dot(combined, w_output, preferred_element_type=jnp.float32)
    return (activations.astype(jnp.float32) + projected).astype(jnp.bfloat16)


def solution(mesh):
    in_specs = (P(("sx", "sy"), None), P(), P(), P(), P(), P(("sx", "sy"), None))
    out_specs = P(("sx", "sy"), None)
    return jax.shard_map(body, mesh=mesh, in_specs=in_specs, out_specs=out_specs, check_vma=False)
```

profile of v0, /device:TPU:1, one launch (start us, length us, event | category | flops | bytes accessed | tf_op | source)
XLA Modules:
  0.0 285.0 jit_solution(1354022651606575120)
XLA Ops:
  1.8 11.5 %all-to-all-start = ((s32[128,1,2]{2,1,0:T(1,128)}), s32[128,1,2]{2,1,0:T(1,128)S(1)}, u32[]{:S(2)}, u32[]{:S(2)}) async-start(s32[128,1,2]{2,1,0:T(1,128)} %bitcast.5), calls=%async_computation | async-start | bytes 131072 | tf_op jit(solution)/shard_map/all_to_all | solution.py:168
  18.9 6.6 %convolution_convert_fusion = bf16[512,3072]{1,0:T(8,128)(2,1)S(1)} fusion(bf16[1024,3072]{1,0:T(8,128)(2,1)} %param.11, bf16[512,1024]{1,0:T(8,128)(2,1)} %param.8, f32[1024]{0:T(1024)} %param.9, f32[512]{0:T(512)S(1)} %add_rsqrt_fusion), kind=kOutput, calls=%fused_computation.21 | convolution fusion | flops 3224895488 | bytes 10491904 | tf_op jit(solution)/shard_map/dot_general | solution.py:149
  25.5 4.4 %fusion.20 = bf16[8,640,384]{2,1,0:T(8,128)(2,1)} fusion(bf16[64,8,8,384]{3,2,1,0:T(8,128)(2,1)S(1)} %bitcast.67, s32[8,512]{1,0:T(8,128)S(1)} %fusion.53), kind=kOutput, calls=%fused_computation.32 | convolution fusion | flops 2017853440 | bytes 7094272 | tf_op jit(solution)/shard_map/hst,thf->hsf/dot_general | solution.py:123
  29.9 10.2 %all-to-all-start.1 = ((bf16[128,40,384]{2,1,0:T(8,128)(2,1)}), bf16[128,40,384]{2,1,0:T(8,128)(2,1)}, u32[]{:S(2)}, u32[]{:S(2)}) async-start(bf16[128,40,384]{2,1,0:T(8,128)(2,1)} %bitcast.62), calls=%async_computation.1 | async-start | bytes 7864320 | tf_op jit(solution)/shard_map/all_to_all | solution.py:167
  40.1 3.1 %convolution_convert_fusion.1 = bf16[512,1536]{1,0:T(8,128)(2,1)S(1)} fusion(bf16[1024,1536]{1,0:T(8,128)(2,1)S(1)} %copy-done, bf16[512,1024]{1,0:T(8,128)(2,1)} %param.8, f32[1024]{0:T(1024)S(1)} %copy-done.5, f32[512]{0:T(512)S(1)} %add_rsqrt_fusion), kind=kOutput, calls=%fused_computation.31 | convolution fusion | flops 1613496320 | bytes 5773312 | tf_op jit(solution)/shard_map/dot_general | solution.py:148
  45.5 3.7 %collective-permute-start = (bf16[512,1024]{1,0:T(8,128)(2,1)}, bf16[512,1024]{1,0:T(8,128)(2,1)}, u32[]{:S(2)}, u32[]{:S(2)}) collective-permute-start(bf16[512,1024]{1,0:T(8,128)(2,1)} %slice.31), channel_id=1, source_target_pairs={{0,1},{1,2},{2,3},{3,4},{4,5},{5,6},{6,7},{7,8},{8,9},{9,10},{10,1... | collective-permute-start | bytes 3145736 | tf_op jit(solution)/shard_map/ppermute | solution.py:19
  51.2 42.2 %collective-permute-done = bf16[512,1024]{1,0:T(8,128)(2,1)} collective-permute-done((bf16[512,1024]{1,0:T(8,128)(2,1)}, bf16[512,1024]{1,0:T(8,128)(2,1)}, u32[]{:S(2)}, u32[]{:S(2)}) %collective-permute-start) | collective-permute-done | bytes 1048608 | tf_op jit(solution)/shard_map/ppermute | solution.py:19
  93.3 2.7 fusion.42
  96.1 5.6 %fusion.39 = f32[4,512,1024]{2,1,0:T(8,128)} fusion(bf16[128,4,8,128]{3,2,1,0:T(8,128)(2,1)S(1)} %get-tuple-element.84, bf16[512,1536]{1,0:T(8,128)(2,1)} %copy-done.1), kind=kOutput, calls=%fused_computation.53 | convolution fusion | flops 536870912 | bytes 9961472 | tf_op jit(solution)/shard_map/while/body/eval_jaxpr/qhd,khd->hqk/dot_general | solution.py:46
  101.7 4.1 %fusion.59 = (bf16[5120,128]{1,0:T(8,128)(2,1)}, bf16[5120,128]{1,0:T(8,128)(2,1)}, bf16[5120,128]{1,0:T(8,128)(2,1)}) fusion(bf16[5120,384]{1,0:T(8,128)(2,1)} %bitcast.13), kind=kLoop, calls=%fused_computation.90 | loop fusion | bytes 7864320 | tf_op jit(solution)/shard_map/slice | solution.py:73
  105.8 135.6 %while.2 = (s32[]{:T(128)}, bf16[16,320,128]{2,1,0:T(8,128)(2,1)}, s32[16]{0:T(128)S(1)}, s32[5120]{0:T(1024)S(1)}, s32[5120]{0:T(1024)S(1)}, /*index=5*/bf16[51...) while((s32[]{:T(128)}, bf16[16,320,128]{2,1,0:T(8,128)(2,1)}, ...), condition=%wide.region_12.13_spmd, body=%wide.region_9.12_spmd.sunk | while | flops 853646720 | bytes 27719884 | solution.py:87
  108.4 2.7 fusion.76
  116.9 2.7 fusion.76
  150.8 2.7 fusion.76
  167.8 2.7 fusion.76
  176.3 2.7 fusion.76
  201.7 2.7 fusion.76
  210.2 2.7 fusion.76
  241.5 3.7 %broadcast_select_fusion = bf16[128,40,128]{2,1,0:T(8,128)(2,1)} fusion(bf16[128,40,128]{2,1,0:T(8,128)(2,1)} %bitcast.63, pred[128,40]{1,0:T(8,128)(4,1)S(1)} %copy.27), kind=kLoop, calls=%fused_computation.48 | loop fusion | flops 655360 | bytes 2626560 | tf_op jit(solution)/shard_map/jit(_where)/select_n | solution.py:101
  245.2 11.4 %all-to-all-start.2 = ((bf16[128,40,128]{2,1,0:T(8,128)(2,1)}), bf16[128,40,128]{2,1,0:T(8,128)(2,1)}, u32[]{:S(2)}, u32[]{:S(2)}) async-start(bf16[128,40,128]{2,1,0:T(8,128)(2,1)} %broadcast_select_fusion), calls=%async_computation.2 | async-start | bytes 2621440 | tf_op jit(solution)/shard_map/all_to_all | solution.py:171
  256.6 13.5 %fusion.60 = (f32[4,512]{1,0:T(4,128)S(1)}, f32[4,512,1024]{2,1,0:T(8,128)}) fusion(f32[4,512,1024]{2,1,0:T(8,128)} %fusion.39, pred[512,1024]{1,0:T(8,128)(4,1)} %fusion.28), kind=kOutput, calls=%fused_computation.91 | output fusion | flops 12583935 | bytes 17309696 | tf_op jit(solution)/shard_map/while/body/eval_jaxpr/sub | solution.py:30
  272.4 6.1 %fusion.36 = bf16[4,128,512]{2,1,0:T(8,128)(2,1)} fusion(bf16[1024,4,128]{0,2,1:T(8,128)(2,1)} %bitcast.64, f32[4,512,1024]{2,1,0:T(8,128)} %get-tuple-element.87, f32[4,512]{1,0:T(4,128)S(1)} %get-tuple-element.86), kind=kOutput, calls=%fused_computation.49 | convolution fusion | flops 541327360 | bytes 9969664 | tf_op jit(solution)/shard_map/while/body/eval_jaxpr/hqk,khd->qhd/dot_general | solution.py:58
  278.5 3.6 %fusion.33 = bf16[8,128,512]{2,1,0:T(8,128)(2,1)S(1)} fusion(bf16[8,640,128]{2,1,0:T(8,128)(2,1)} %bitcast.15, s32[8,512]{1,0:T(8,128)S(1)} %fusion.53), kind=kOutput, calls=%fused_computation.47 | convolution fusion | flops 674234368 | bytes 2375680 | tf_op jit(solution)/shard_map/hst,hsf->thf/dot_general | solution.py:131
  282.2 2.8 fusion.26
  (149 shorter events, 99.2 us)
Async XLA Ops:
  0.0 40.1 %copy-start = (bf16[1024,1536]{1,0:T(8,128)(2,1)S(1)}, bf16[1024,1536]{1,0:T(8,128)(2,1)}, u32[]{:S(2)}) copy-start(bf16[1024,1536]{1,0:T(8,128)(2,1)} %param.10) | copy-start | bytes 9437188
  1.8 28.1 %all-to-all-start = ((s32[128,1,2]{2,1,0:T(1,128)}), s32[128,1,2]{2,1,0:T(1,128)S(1)}, u32[]{:S(2)}, u32[]{:S(2)}) async-start(s32[128,1,2]{2,1,0:T(1,128)} %bitcast.5), calls=%async_computation | async-start | bytes 131072 | tf_op jit(solution)/shard_map/all_to_all | solution.py:168
  29.9 10.2 %copy-start.5 = (f32[1024]{0:T(1024)S(1)}, f32[1024]{0:T(1024)}, u32[]{:S(2)}) copy-start(f32[1024]{0:T(1024)} %param.9) | copy-start | bytes 12292
  29.9 71.8 %all-to-all-start.1 = ((bf16[128,40,384]{2,1,0:T(8,128)(2,1)}), bf16[128,40,384]{2,1,0:T(8,128)(2,1)}, u32[]{:S(2)}, u32[]{:S(2)}) async-start(bf16[128,40,384]{2,1,0:T(8,128)(2,1)} %bitcast.62), calls=%async_computation.1 | async-start | bytes 7864320 | tf_op jit(solution)/shard_map/all_to_all | solution.py:167
  45.5 47.8 %collective-permute-start = (bf16[512,1024]{1,0:T(8,128)(2,1)}, bf16[512,1024]{1,0:T(8,128)(2,1)}, u32[]{:S(2)}, u32[]{:S(2)}) collective-permute-start(bf16[512,1024]{1,0:T(8,128)(2,1)} %slice.31), channel_id=1, source_target_pairs={{0,1},{1,2},{2,3},{3,4},{4,5},{5,6},{6,7},{7,8},{8,9},{9,10},{10,1... | collective-permute-start | bytes 3145736 | tf_op jit(solution)/shard_map/ppermute | solution.py:19
  111.1 1.3 copy-start.2
  119.6 1.3 copy-start.2
  128.1 1.3 copy-start.2
  136.6 1.3 copy-start.2
  145.0 1.3 copy-start.2
  153.5 1.3 copy-start.2
  162.0 1.3 copy-start.2
  170.5 1.3 copy-start.2
  179.0 1.3 copy-start.2
  187.4 1.3 copy-start.2
  195.9 1.3 copy-start.2
  204.4 1.3 copy-start.2
  212.9 1.3 copy-start.2
  229.8 1.3 copy-start.2
  238.3 1.3 copy-start.2
  245.2 33.3 %all-to-all-start.2 = ((bf16[128,40,128]{2,1,0:T(8,128)(2,1)}), bf16[128,40,128]{2,1,0:T(8,128)(2,1)}, u32[]{:S(2)}, u32[]{:S(2)}) async-start(bf16[128,40,128]{2,1,0:T(8,128)(2,1)} %broadcast_select_fusion), calls=%async_computation.2 | async-start | bytes 2621440 | tf_op jit(solution)/shard_map/all_to_all | solution.py:171
  278.5 3.7 %copy-start.3 = (bf16[512,1024]{1,0:T(8,128)(2,1)S(1)}, bf16[512,1024]{1,0:T(8,128)(2,1)}, u32[]{:S(2)}) copy-start(bf16[512,1024]{1,0:T(8,128)(2,1)} %param.8) | copy-start | bytes 3145732
  278.5 3.7 %copy-start.4 = (bf16[1536,1024]{1,0:T(8,128)(2,1)S(1)}, bf16[1536,1024]{1,0:T(8,128)(2,1)}, u32[]{:S(2)}) copy-start(bf16[1536,1024]{1,0:T(8,128)(2,1)} %param.12) | copy-start | bytes 9437188
  278.5 3.7 %copy-start.6 = (bf16[4,128,512]{2,1,0:T(8,128)(2,1)S(1)}, bf16[4,128,512]{2,1,0:T(8,128)(2,1)}, u32[]{:S(2)}) copy-start(bf16[4,128,512]{2,1,0:T(8,128)(2,1)} %fusion.36) | copy-start | bytes 1572868
  (2 other events, 2.5 us)
where the time goes:
time: 287 us; the launch traced here: 285 us
  matrix products  106 us (37%)
  other arithmetic  43.3 us (15%)
  waiting for transfers between devices  42.2 us (15%)
  starting transfers between devices  36.8 us (13%)
  loops' own time  31.3 us (11%)
  local copies, waits for them, and re-layouts  25 us (9%)
    dot_general x16, matrix products, tagged_one_block(): jnp.einsum('qd,kd->qk', query_block, key_rows, preferred_element_type=jnp...  43.2 us
    ppermute x1, waiting for transfers between devices, shifted(): lax.ppermute(value, axis, [(source, source + steps) for source in range(l...  42.2 us
    another operation x1, loops' own time, tagged_attention(): return lax.map(tagged_one_block, starts).reshape(total, HD)  31.3 us
    dot_general x16, matrix products, tagged_one_block(): jnp.dot(weights, value_rows, preferred_element_type=jnp.float32)  29.5 us
    reduce_sum x16, other arithmetic, normalize_rows(): jnp.sum(raised, axis=-1, keepdims=True)  16.7 us
    sub x1, other arithmetic, normalize_rows(): raised = jnp.exp(scores - highest)  13.5 us
    all_to_all x1, starting transfers between devices, body(): lax.all_to_all(send_counts, ('sx', 'sy'), split_axis=0, concat_axis=0, ti...  11.5 us
    all_to_all x1, starting transfers between devices, body(): lax.all_to_all(finished, ('sx', 'sy'), split_axis=0, concat_axis=0, tiled...  11.4 us
  transfers between devices with their start and end apart: 4, of which 1 were waited for; matrix products, arithmetic and copies ran while one was open for 19% of the time, Pallas kernels for 0%

commit v1 on v0

v1 whole, which is shorter than its diff:
```python
import functools
import math

import jax
import jax.numpy as jnp
from jax import lax
from jax.experimental import pallas as pl
from jax.experimental.pallas import tpu as pltpu
from jax.sharding import PartitionSpec as P

HL = 4
HC = 8
HD = 128
WIN = 512
CSIZE = 2048
CLUSTERS = 32
TOK = 512
D = 1024
SHARDS = 128
POOL = 40
PER_CLUSTER = 28
GROUPS = CLUSTERS // 2
REGION = GROUPS * POOL
CHUNK = 8
CHUNKS = SHARDS // CHUNK
CHUNK_ROWS = CHUNK * POOL
SPAN = CHUNK * PER_CLUSTER + 16
QBLOCK = 256
EPSILON = 1e-06
AXES = ("sx", "sy")
VMEM = 60 * 2**20
EXP2_SCALE = HD ** (-0.5) * math.log2(math.e)
NT = (((1,), (1,)), ((), ()))
TN = (((0,), (0,)), ((), ()))
F32 = jnp.float32
BF16 = jnp.bfloat16


def iota(shape, dim):
    return lax.broadcasted_iota(jnp.int32, shape, dim)


def one_hot(condition):
    return jnp.where(condition, 1.0, 0.0).astype(BF16)


def rms_norm(activations, norm_gain):
    values = activations.astype(F32)
    mean_square = jnp.mean(values * values, axis=-1, keepdims=True)
    return (values * lax.rsqrt(mean_square + EPSILON) * norm_gain).astype(BF16)


def slot_of(cluster, position):
    return (cluster >> 1) * POOL + jnp.where((cluster & 1) == 1, POOL - 1 - position, position)


def pre_kernel(act_ref, gain_ref, w_ref, asg_ref, out_ref, normed, slots):
    head = pl.program_id(0)

    @pl.when(head == 0)
    def _():
        normed[...] = rms_norm(act_ref[...], gain_ref[...])
        asg = asg_ref[...].astype(F32).astype(BF16)
        spread = one_hot((iota((HC * CLUSTERS, HC), 0) >> 5) == iota((HC * CLUSTERS, HC), 1))
        value = lax.dot_general(spread, asg, NT, preferred_element_type=F32)
        member = value == (iota((HC * CLUSTERS, TOK), 0) & (CLUSTERS - 1)).astype(F32)
        before = one_hot(iota((TOK, TOK), 0) < iota((TOK, TOK), 1))
        running = jnp.dot(one_hot(member), before, preferred_element_type=F32)
        gather = one_hot(iota((HC, HC * CLUSTERS), 0) == (iota((HC, HC * CLUSTERS), 1) >> 5))
        position = jnp.dot(
            gather, jnp.where(member, running, 0.0).astype(BF16), preferred_element_type=F32
        ).astype(jnp.int32)
        eye = one_hot(iota((HC, HC), 0) == iota((HC, HC), 1))
        cluster = lax.dot_general(eye, asg, NT, preferred_element_type=F32).astype(jnp.int32)
        slot = slot_of(cluster, position)
        for index in range(HC):
            slots[index] = slot[index : index + 1]

    qkv = jnp.dot(normed[...], w_ref[...], preferred_element_type=F32).astype(BF16)
    table = one_hot(iota((REGION, TOK), 0) == slots[head])
    out_ref[...] = jnp.dot(table, qkv, preferred_element_type=F32).astype(BF16)


def pre_call(activations, norm_gain, w_cluster, assignment):
    return pl.pallas_call(
        pre_kernel,
        grid=(HC,),
        in_specs=[
            pl.BlockSpec((TOK, D), lambda h: (0, 0)),
            pl.BlockSpec((1, D), lambda h: (0, 0)),
            pl.BlockSpec((D, 3 * HD), lambda h: (0, h)),
            pl.BlockSpec((TOK, HC), lambda h: (0, 0)),
        ],
        out_specs=pl.BlockSpec((REGION, 3 * HD), lambda h: (h, 0)),
        out_shape=jax.ShapeDtypeStruct((SHARDS * POOL, 3 * HD), BF16),
        scratch_shapes=[pltpu.VMEM((TOK, D), BF16), pltpu.VMEM((HC, 1, TOK), jnp.int32)],
        compiler_params=pltpu.CompilerParams(vmem_limit_bytes=VMEM),
        name="place",
    )(activations, norm_gain.reshape(1, D), w_cluster, assignment)


def softmax_rows(scores):
    highest = jnp.max(scores, axis=-1, keepdims=True)
    raised = jnp.exp2((scores - highest) * EXP2_SCALE)
    total = jnp.sum(raised, axis=-1, keepdims=True)
    return (raised * (1.0 / total)).astype(BF16)


def window_kernel(first_ref, qkv_ref, rim_ref, act_ref, w_ref, out_ref, mix):
    width = HL * HD
    step = 128
    shift = jnp.where(first_ref[0] == 0, WIN, 0)
    for head in range(HL):
        lanes = slice(head * HD, (head + 1) * HD)
        key_lanes = slice(width + head * HD, width + (head + 1) * HD)
        value_lanes = slice(2 * width + head * HD, 2 * width + (head + 1) * HD)
        for low in range(0, TOK, step):
            high = low + step
            query = qkv_ref[low:high, lanes]
            keys = jnp.concatenate([rim_ref[low:, lanes], qkv_ref[:high, key_lanes]], axis=0)
            values = jnp.concatenate(
                [rim_ref[low:, key_lanes], qkv_ref[:high, value_lanes]], axis=0
            )
            scores = lax.dot_general(query, keys, NT, preferred_element_type=F32)
            rows = iota(scores.shape, 0)
            cols = iota(scores.shape, 1)
            allowed = (cols > rows) & (cols <= rows + WIN) & (cols + low >= shift)
            weights = softmax_rows(jnp.where(allowed, scores, -1e30))
            mix[low:high, lanes] = jnp.dot(weights, values, preferred_element_type=F32).astype(BF16)
    out_ref[...] = act_ref[...].astype(F32) + jnp.dot(
        mix[...], w_ref[...], preferred_element_type=F32
    )


def window_call(first, local_qkv, rim, activations, w_output):
    width = HL * HD
    return pl.pallas_call(
        window_kernel,
        grid=(1,),
        in_specs=[
            pl.BlockSpec(memory_space=pltpu.SMEM),
            pl.BlockSpec((TOK, 3 * width), lambda i: (0, 0)),
            pl.BlockSpec((WIN, 2 * width), lambda i: (0, 0)),
            pl.BlockSpec((TOK, D), lambda i: (0, 0)),
            pl.BlockSpec((width, D), lambda i: (0, 0)),
        ],
        out_specs=pl.BlockSpec((TOK, D), lambda i: (0, 0)),
        out_shape=jax.ShapeDtypeStruct((TOK, D), F32),
        scratch_shapes=[pltpu.VMEM((TOK, width), BF16)],
        compiler_params=pltpu.CompilerParams(vmem_limit_bytes=VMEM),
        cost_estimate=pl.CostEstimate(flops=10**10, bytes_accessed=10**7, transcendentals=0),
        name="window",
    )(first, local_qkv, rim, activations, w_output)


def cluster_kernel(base_ref, pool_ref, rel_ref, out_ref, packed, mixed):
    packed[:, :16] = jnp.zeros((2, 16, 3 * HD), BF16)
    mixed[:, CSIZE:] = jnp.zeros((2, SPAN, HD), BF16)

    @pl.loop(0, CHUNKS)
    def _(chunk):
        rows = pool_ref[pl.ds(pl.multiple_of(chunk * CHUNK_ROWS, 16), CHUNK_ROWS), :]
        for which in range(2):
            index = chunk * 2 + which
            base = pl.multiple_of(base_ref[index], 16)
            table = one_hot(iota((SPAN, CHUNK_ROWS), 0) == rel_ref[index])
            moved = jnp.dot(table, rows, preferred_element_type=F32).astype(BF16)
            packed[which, pl.ds(base, 16), :] += moved[:16]
            packed[which, pl.ds(pl.multiple_of(base + 16, 16), SPAN - 16), :] = moved[16:]

    for which in range(2):

        @pl.loop(0, CSIZE // QBLOCK)
        def _(block):
            place = pl.ds(pl.multiple_of(block * QBLOCK, QBLOCK), QBLOCK)
            query = packed[which, place, :HD]
            scores = lax.dot_general(
                query, packed[which, :CSIZE, HD : 2 * HD], NT, preferred_element_type=F32
            )
            weights = softmax_rows(scores)
            mixed[which, place, :] = jnp.dot(
                weights, packed[which, :CSIZE, 2 * HD :], preferred_element_type=F32
            ).astype(BF16)

    @pl.loop(0, CHUNKS)
    def _(chunk):
        total = jnp.zeros((CHUNK_ROWS, HD), F32)
        for which in range(2):
            index = chunk * 2 + which
            base = pl.multiple_of(base_ref[index], 16)
            table = one_hot(iota((SPAN, CHUNK_ROWS), 0) == rel_ref[index])
            total += lax.dot_general(
                table, mixed[which, pl.ds(base, SPAN), :], TN, preferred_element_type=F32
            )
        out_ref[pl.ds(pl.multiple_of(chunk * CHUNK_ROWS, 16), CHUNK_ROWS), :] = total.astype(BF16)


def cluster_call(bases, pool, rel):
    return pl.pallas_call(
        cluster_kernel,
        in_specs=[
            pl.BlockSpec(memory_space=pltpu.SMEM),
            pl.BlockSpec(memory_space=pltpu.VMEM),
            pl.BlockSpec(memory_space=pltpu.VMEM),
        ],
        out_specs=pl.BlockSpec(memory_space=pltpu.VMEM),
        out_shape=jax.ShapeDtypeStruct((SHARDS * POOL, HD), BF16),
        scratch_shapes=[
            pltpu.VMEM((2, CSIZE + SPAN, 3 * HD), BF16),
            pltpu.VMEM((2, CSIZE + SPAN, HD), BF16),
        ],
        compiler_params=pltpu.CompilerParams(vmem_limit_bytes=VMEM),
        name="cluster",
    )(bases, pool, rel)


def post_kernel(back_ref, slot_ref, base_ref, w_ref, out_ref, total):
    step = pl.program_id(0)

    @pl.when(step == 0)
    def _():
        total[...] = base_ref[...]

    parts = []
    for inner in range(2):
        pick = iota((TOK, HC), 1) == step * 2 + inner
        slot = jnp.sum(jnp.where(pick, slot_ref[...], 0), axis=1, keepdims=True)
        table = one_hot(iota((TOK, REGION), 1) == slot)
        rows = back_ref[inner * REGION : (inner + 1) * REGION, :]
        parts.append(jnp.dot(table, rows, preferred_element_type=F32).astype(BF16))
    mix = jnp.concatenate(parts, axis=1)
    total[...] += jnp.dot(mix, w_ref[...], preferred_element_type=F32)

    @pl.when(step == HC // 2 - 1)
    def _():
        out_ref[...] = total[...].astype(BF16)


def post_call(back, slot, base, w_output):
    return pl.pallas_call(
        post_kernel,
        grid=(HC // 2,),
        in_specs=[
            pl.BlockSpec((2 * REGION, HD), lambda h: (h, 0)),
            pl.BlockSpec((TOK, HC), lambda h: (0, 0)),
            pl.BlockSpec((TOK, D), lambda h: (0, 0)),
            pl.BlockSpec((2 * HD, D), lambda h: (h + HL // 2, 0)),
        ],
        out_specs=pl.BlockSpec((TOK, D), lambda h: (0, 0)),
        out_shape=jax.ShapeDtypeStruct((TOK, D), BF16),
        scratch_shapes=[pltpu.VMEM((TOK, D), F32)],
        compiler_params=pltpu.CompilerParams(vmem_limit_bytes=VMEM),
        name="collect",
    )(back, slot, base, w_output)


def token_slots(assignment):
    member = assignment[:, :, None] == jnp.arange(CLUSTERS, dtype=jnp.int32)
    rows = jnp.arange(TOK, dtype=jnp.int32)
    earlier = (rows[:, None] > rows[None, :]).astype(BF16)
    running = jnp.dot(
        earlier, member.astype(BF16).reshape(TOK, HC * CLUSTERS), preferred_element_type=F32
    ).reshape(TOK, HC, CLUSTERS)
    position = jnp.sum(jnp.where(member, running, 0.0), axis=2).astype(jnp.int32)
    return slot_of(assignment, position)


def compaction_plan(counts):
    sources = jnp.arange(SHARDS, dtype=jnp.int32)
    earlier = (sources[:, None] > sources[None, :]).astype(BF16)
    start = jnp.dot(earlier, counts.astype(BF16), preferred_element_type=F32).astype(jnp.int32)
    bases = start.reshape(CHUNKS, CHUNK, 2)[:, 0, :] // 16 * 16
    local = (start.reshape(CHUNKS, CHUNK, 2) - bases[:, None, :]).reshape(SHARDS, 2)
    places = jnp.arange(POOL, dtype=jnp.int32)
    order = jnp.stack([places, POOL - 1 - places])
    inside = order[None] < counts[:, :, None]
    rel = jnp.where(inside, local[:, :, None] + order[None], -1)
    rel = rel.reshape(CHUNKS, CHUNK, 2, POOL).transpose(0, 2, 1, 3)
    return bases.reshape(2 * CHUNKS), rel.reshape(2 * CHUNKS, 1, CHUNK_ROWS)


def body(activations, norm_gain, w_local, w_cluster, w_output, assignment):
    device = lax.axis_index(AXES)
    member = assignment[:, :, None] == jnp.arange(CLUSTERS, dtype=jnp.int32)
    counts = jnp.sum(member.astype(jnp.int32), axis=0).reshape(SHARDS, 2)
    got_counts = lax.all_to_all(counts, AXES, split_axis=0, concat_axis=0, tiled=True)

    placed = pre_call(activations, norm_gain, w_cluster, assignment)
    placed, got_counts = lax.optimization_barrier((placed, got_counts))
    got_pool = lax.all_to_all(
        placed.reshape(SHARDS, POOL, 3 * HD), AXES, split_axis=0, concat_axis=0, tiled=True
    )

    local_qkv = jnp.dot(
        rms_norm(activations, norm_gain), w_local, preferred_element_type=F32
    ).astype(BF16)
    slot = token_slots(assignment)
    bases, rel = compaction_plan(got_counts)

    got_pool, local_kv, bases, rel, slot = lax.optimization_barrier(
        (got_pool, local_qkv[:, HL * HD :], bases, rel, slot)
    )
    rim = lax.ppermute(local_kv, AXES, [(i, i + 1) for i in range(SHARDS - 1)])
    finished = cluster_call(bases, got_pool.reshape(SHARDS * POOL, 3 * HD), rel)
    finished, rim = lax.optimization_barrier((finished, rim))
    came_back = lax.all_to_all(
        finished.reshape(SHARDS, POOL, HD), AXES, split_axis=0, concat_axis=0, tiled=True
    )
    base = window_call(
        jnp.minimum(device, 1).astype(jnp.int32).reshape(1), local_qkv, rim, activations, w_output
    )
    return post_call(came_back.reshape(SHARDS * POOL, HD), slot, base, w_output)


def solution(mesh):
    in_specs = (P(AXES, None), P(), P(), P(), P(), P(AXES, None))
    out_specs = P(AXES, None)
    return jax.shard_map(body, mesh=mesh, in_specs=in_specs, out_specs=out_specs, check_vma=False)
```

time: 287 us -> 161 us (0.56)
  matrix products: 106 us -> 3.66 us
  Pallas kernels: 0 us -> 64.6 us
  other arithmetic: 43.3 us -> 4.33 us
  loops' own time: 31.3 us -> 0 us
  local copies, waits for them, and re-layouts: 25 us -> 7.34 us
  waiting for transfers between devices: 42.2 us -> 48.5 us
  starting transfers between devices: 36.8 us -> 31.7 us
    dot_general x40 -> x3, matrix products: 106 us -> 3.66 us  [the longest x1 3.12 us: body(): jnp.dot(rms_norm(activations, norm_gain), w_local, preferred_element_type...]
    pallas_call x0 -> x4, Pallas kernels: none -> 64.6 us  [the longest x1 33.7 us: cluster_call(): pl.pallas_call(cluster_kernel, in_specs=[pl.BlockSpec(memory_space=pltpu....]
    all_to_all x3, waiting for transfers between devices: 0.01 us -> 48.5 us  [the longest x1 37.9 us: body(): lax.all_to_all(placed.reshape(SHARDS, POOL, 3 * HD), AXES, split_axis=0,...]
    ppermute x1, waiting for transfers between devices: 42.2 us -> 0.01 us  [body(): rim = lax.ppermute(local_kv, AXES, [(i, i + 1) for i in range(SHARDS - 1)])]
    another operation x1 -> x0, loops' own time: 31.3 us -> none  [tagged_attention(): return lax.map(tagged_one_block, starts).reshape(total, HD)]
    reduce_sum x19 -> x1, other arithmetic: 18.7 us -> 1.09 us  [body(): counts = jnp.sum(member.astype(jnp.int32), axis=0).reshape(SHARDS, 2)]
    sub x2 -> x3, other arithmetic: 13.5 us -> 0.02 us  [the longest x1 0.01 us: slot_of(): POOL - 1 - position]
    dynamic_slice x32 -> x0, local copies, waits for them, and re-layouts: 10.6 us -> none  [the longest x16 9.31 us: tagged_attention(): return lax.map(tagged_one_block, starts).reshape(total, HD)]
  transfers between devices with their start and end apart: 4 -> 4, of which waited for: 1 -> 2; matrix products, arithmetic and copies ran while one was open for 19% -> 8% of each run, Pallas kernels for 0% -> 36%
where the time goes in v1:
time: 161 us; the launch traced here: 160 us
  Pallas kernels  64.6 us (40%)
  waiting for transfers between devices  48.5 us (30%)
  starting transfers between devices  31.7 us (20%)
  local copies, waits for them, and re-layouts  7.34 us (5%)
  other arithmetic  4.33 us (3%)
  matrix products  3.66 us (2%)
    all_to_all x1, waiting for transfers between devices, body(): lax.all_to_all(placed.reshape(SHARDS, POOL, 3 * HD), AXES, split_axis=0,...  37.9 us
    pallas_call x1, Pallas kernels, cluster_call(): pl.pallas_call(cluster_kernel, in_specs=[pl.BlockSpec(memory_space=pltpu....  33.7 us
    pallas_call x1, Pallas kernels, pre_call(): pl.pallas_call(pre_kernel, grid=(HC,), in_specs=[pl.BlockSpec((TOK, D), l...  12.8 us
    all_to_all x1, starting transfers between devices, body(): lax.all_to_all(counts, AXES, split_axis=0, concat_axis=0, tiled=True)  11.5 us
    pallas_call x1, Pallas kernels, window_call(): pl.pallas_call(window_kernel, grid=(1,), in_specs=[pl.BlockSpec(memory_sp...  10.8 us
    all_to_all x1, waiting for transfers between devices, body(): lax.all_to_all(finished.reshape(SHARDS, POOL, HD), AXES, split_axis=0, co...  10.6 us
    all_to_all x1, starting transfers between devices, body(): lax.all_to_all(placed.reshape(SHARDS, POOL, 3 * HD), AXES, split_axis=0,...  10.2 us
    pallas_call x1, Pallas kernels, post_call(): pl.pallas_call(post_kernel, grid=(HC // 2,), in_specs=[pl.BlockSpec((2 *...  7.32 us
  transfers between devices with their start and end apart: 4, of which 2 were waited for; matrix products, arithmetic and copies ran while one was open for 8% of the time, Pallas kernels for 36%

profile of v1, /device:TPU:1, one launch (start us, length us, event | category | flops | bytes accessed | tf_op | source)
XLA Modules:
  0.0 160.4 jit_solution(16855131443118498346)
XLA Ops:
  0.0 1.1 convert_reduce_fusion
  1.1 0.7 all_to_all.14
  1.8 11.5 %all-to-all-start = ((s32[128,1,2]{2,1,0:T(1,128)}), s32[128,1,2]{2,1,0:T(1,128)S(1)}, u32[]{:S(2)}, u32[]{:S(2)}) async-start(s32[128,1,2]{2,1,0:T(1,128)} %bitcast.1), calls=%async_computation | async-start | bytes 131072 | tf_op jit(solution)/shard_map/all_to_all | solution.py:286
  13.3 1.5 copy.46.asg_ref
  14.9 12.8 %place.1 = bf16[5120,384]{1,0:T(8,128)(2,1)} custom-call(bf16[512,1024]{1,0:T(8,128)(2,1)} %act_ref.3, f32[1,1024]{1,0:T(1,128)} %bitcast.39, bf16[1024,3072]{1,0:T(8,128)(2,1)} %w_ref.3, s32[512,8]{1,0:T(8,128)} %copy.46.asg_ref), custom_call_target="tpu_custom_call" | custom-call | tf_op jit(solution)/shard_map/place/pallas_call | solution.py:85
  27.7 10.2 %all-to-all-start.1 = ((bf16[128,40,384]{2,1,0:T(8,128)(2,1)}), bf16[128,40,384]{2,1,0:T(8,128)(2,1)}, u32[]{:S(2)}, u32[]{:S(2)}) async-start(bf16[128,40,384]{2,1,0:T(8,128)(2,1)} %bitcast.33), calls=%async_computation.1 | async-start | bytes 7864320 | tf_op jit(solution)/shard_map/all_to_all | solution.py:290
  38.1 0.4 fusion.3
  38.6 0.8 copy.55
  39.5 0.8 copy.56
  40.3 1.5 fusion
  41.8 3.1 %convolution_convert_fusion.qkv_ref = bf16[512,1536]{1,0:T(8,128)(2,1)S(1)} fusion(bf16[1024,1536]{1,0:T(8,128)(2,1)S(1)} %copy-done, bf16[512,1024]{1,0:T(8,128)(2,1)} %act_ref.3, f32[1024]{0:T(1024)S(1)} %copy-done.6, f32[512]{0:T(512)S(1)} %add_rsqrt_fusion), kind=kOutput, calls=%fused_computation | convolution fusion | flops 1613496320 | bytes 5773312 | tf_op jit(solution)/shard_map/dot_general | solution.py:294
  45.0 1.1 slice.8
  46.2 0.2 copy-done.2
  46.4 0.3 copy-done.3
  46.7 0.7 select_add_fusion.slot_ref
  48.4 0.8 select_n.34.rel_ref
  49.5 0.5 fusion.14.base_ref
  50.0 37.9 %all-to-all-done.1 = bf16[128,40,384]{2,1,0:T(8,128)(2,1)} async-done(((bf16[128,40,384]{2,1,0:T(8,128)(2,1)}), bf16[128,40,384]{2,1,0:T(8,128)(2,1)}, u32[]{:S(2)}, u32[]{:S(2)}) %all-to-all-start.1) | async-done | bytes 3932192 | tf_op jit(solution)/shard_map/all_to_all | solution.py:290
  87.9 2.8 %collective-permute-start = (bf16[512,1024]{1,0:T(8,128)(2,1)}, bf16[512,1024]{1,0:T(8,128)(2,1)}, u32[]{:S(2)}, u32[]{:S(2)}) collective-permute-start(bf16[512,1024]{1,0:T(8,128)(2,1)} %slice.8), channel_id=1, source_target_pairs={{0,1},{1,2},{2,3},{3,4},{4,5},{5,6},{6,7},{7,8},{8,9},{9,10},{10,1... | collective-permute-start | bytes 3145736 | tf_op jit(solution)/shard_map/ppermute | solution.py:303
  90.8 33.7 %cluster.1 = bf16[5120,128]{1,0:T(8,128)(2,1)} custom-call(s32[32]{0:T(128)} %fusion.14.base_ref, bf16[5120,384]{1,0:T(8,128)(2,1)} %bitcast.12.pool_ref, s32[32,1,320]{2,1,0:T(1,128)} %select_n.34.rel_ref), custom_call_target="tpu_custom_call" | custom-call | tf_op jit(solution)/shard_map/cluster/pallas_call | solution.py:199
  124.5 7.2 %all-to-all-start.2 = ((bf16[128,40,128]{2,1,0:T(8,128)(2,1)}), bf16[128,40,128]{2,1,0:T(8,128)(2,1)}, u32[]{:S(2)}, u32[]{:S(2)}) async-start(bf16[128,40,128]{2,1,0:T(8,128)(2,1)} %bitcast.34), calls=%async_computation.2 | async-start | bytes 2621440 | tf_op jit(solution)/shard_map/all_to_all | solution.py:306
  131.7 10.8 %window.1.base_ref = f32[512,1024]{1,0:T(8,128)} custom-call(s32[1]{0:T(128)} %bitcast.15.first_ref, bf16[512,1536]{1,0:T(8,128)(2,1)} %copy-done.4, bf16[512,1024]{1,0:T(8,128)(2,1)} %collective-permute-done.rim_ref, bf16[512,1024]{1,0:T(8,128)(2,1)} %act_ref.3, bf16[1536,1024]{1,0:T(8,128)(2,1)} %w_ref.5), custom_call_target="tpu_custom_call" | custom-call | flops 10000000000 | bytes 10000000 | tf_op jit(solution)/shard_map/window/pallas_call | solution.py:137
  142.4 10.6 %all-to-all-done.2 = bf16[128,40,128]{2,1,0:T(8,128)(2,1)} async-done(((bf16[128,40,128]{2,1,0:T(8,128)(2,1)}), bf16[128,40,128]{2,1,0:T(8,128)(2,1)}, u32[]{:S(2)}, u32[]{:S(2)}) %all-to-all-start.2) | async-done | bytes 1310752 | tf_op jit(solution)/shard_map/all_to_all | solution.py:306
  153.0 7.3 %collect.1 = bf16[512,1024]{1,0:T(8,128)(2,1)} custom-call(bf16[5120,128]{1,0:T(8,128)(2,1)} %bitcast.14.back_ref, s32[512,8]{1,0:T(8,128)} %select_add_fusion.slot_ref, f32[512,1024]{1,0:T(8,128)} %window.1.base_ref, bf16[1536,1024]{1,0:T(8,128)(2,1)} %w_ref.5), custom_call_target="tpu_custom_call" | custom-call | tf_op jit(solution)/shard_map/collect/pallas_call | solution.py:240
  (37 shorter events, 1.7 us)
Async XLA Ops:
  0.0 41.8 %copy-start = (bf16[1024,1536]{1,0:T(8,128)(2,1)S(1)}, bf16[1024,1536]{1,0:T(8,128)(2,1)}, u32[]{:S(2)}) copy-start(bf16[1024,1536]{1,0:T(8,128)(2,1)} %param.8) | copy-start | bytes 9437188
  1.8 25.9 %all-to-all-start = ((s32[128,1,2]{2,1,0:T(1,128)}), s32[128,1,2]{2,1,0:T(1,128)S(1)}, u32[]{:S(2)}, u32[]{:S(2)}) async-start(s32[128,1,2]{2,1,0:T(1,128)} %bitcast.1), calls=%async_computation | async-start | bytes 131072 | tf_op jit(solution)/shard_map/all_to_all | solution.py:286
  27.7 10.3 %copy-start.5 = (s32[512,8]{0,1:T(8,128)S(1)}, s32[512,8]{0,1:T(8,128)}, u32[]{:S(2)}) copy-start(s32[512,8]{0,1:T(8,128)} %param.11) | copy-start | bytes 49156
  27.7 60.2 %all-to-all-start.1 = ((bf16[128,40,384]{2,1,0:T(8,128)(2,1)}), bf16[128,40,384]{2,1,0:T(8,128)(2,1)}, u32[]{:S(2)}, u32[]{:S(2)}) async-start(bf16[128,40,384]{2,1,0:T(8,128)(2,1)} %bitcast.33), calls=%async_computation.1 | async-start | bytes 7864320 | tf_op jit(solution)/shard_map/all_to_all | solution.py:290
  37.8 4.0 %copy-start.6 = (f32[1024]{0:T(1024)S(1)}, f32[1024]{0:T(1024)}, u32[]{:S(2)}) copy-start(f32[1024]{0:T(1024)} %param.7) | copy-start | bytes 12292
  45.0 2.4 %copy-start.4 = (bf16[512,1536]{1,0:T(8,128)(2,1)}, bf16[512,1536]{1,0:T(8,128)(2,1)S(1)}, u32[]{:S(2)}) copy-start(bf16[512,1536]{1,0:T(8,128)(2,1)S(1)} %convolution_convert_fusion.qkv_ref) | copy-start | bytes 4718596
  45.0 1.2 copy-start.1
  45.0 1.4 copy-start.2
  45.0 1.7 %copy-start.3 = (s32[512,8]{1,0:T(8,128)S(1)}, s32[512,8]{1,0:T(8,128)}, u32[]{:S(2)}) copy-start(s32[512,8]{1,0:T(8,128)} %copy.56) | copy-start | bytes 49156
  87.9 36.6 %collective-permute-start = (bf16[512,1024]{1,0:T(8,128)(2,1)}, bf16[512,1024]{1,0:T(8,128)(2,1)}, u32[]{:S(2)}, u32[]{:S(2)}) collective-permute-start(bf16[512,1024]{1,0:T(8,128)(2,1)} %slice.8), channel_id=1, source_target_pairs={{0,1},{1,2},{2,3},{3,4},{4,5},{5,6},{6,7},{7,8},{8,9},{9,10},{10,1... | collective-permute-start | bytes 3145736 | tf_op jit(solution)/shard_map/ppermute | solution.py:303
  124.5 28.6 %all-to-all-start.2 = ((bf16[128,40,128]{2,1,0:T(8,128)(2,1)}), bf16[128,40,128]{2,1,0:T(8,128)(2,1)}, u32[]{:S(2)}, u32[]{:S(2)}) async-start(bf16[128,40,128]{2,1,0:T(8,128)(2,1)} %bitcast.34), calls=%async_computation.2 | async-start | bytes 2621440 | tf_op jit(solution)/shard_map/all_to_all | solution.py:306

commit v2 on v1

v2 whole, which is shorter than its diff:
```python
import functools
import math

import jax
import jax.numpy as jnp
from jax import lax
from jax.experimental import pallas as pl
from jax.experimental.pallas import tpu as pltpu
from jax.sharding import PartitionSpec as P

HL = 4
HC = 8
HD = 128
WIN = 512
CSIZE = 2048
CLUSTERS = 32
TOK = 512
D = 1024
SHARDS = 128
POOL = 40
PER_CLUSTER = 28
GROUPS = CLUSTERS // 2
REGION = GROUPS * POOL
MAIN = 32
TAIL = POOL - MAIN
PACK = 3 * MAIN + 4 * TAIL
HEADS_STEP = 2
CHUNK = 4
CHUNKS = SHARDS // CHUNK
CHUNK_ROWS = CHUNK * POOL
SPAN = CHUNK * PER_CLUSTER + 16
QBLOCK = 512
EPSILON = 1e-06
AXES = ("sx", "sy")
VMEM = 60 * 2**20
EXP2_SCALE = HD ** (-0.5) * math.log2(math.e)
NT = (((1,), (1,)), ((), ()))
TN = (((0,), (0,)), ((), ()))
F32 = jnp.float32
BF16 = jnp.bfloat16


def iota(shape, dim):
    return lax.broadcasted_iota(jnp.int32, shape, dim)


def one_hot(condition):
    return jnp.where(condition, 1.0, 0.0).astype(BF16)


def rms_norm(activations, norm_gain):
    values = activations.astype(F32)
    mean_square = jnp.mean(values * values, axis=-1, keepdims=True)
    return (values * lax.rsqrt(mean_square + EPSILON) * norm_gain).astype(BF16)


def slot_of(cluster, position):
    return jnp.where((cluster & 1) == 1, POOL - 1 - position, position)


def pre_kernel(act_ref, gain_ref, w_ref, asg_ref, out_ref, normed, rows, sizes):
    step = pl.program_id(0)

    @pl.when(step == 0)
    def _():
        normed[...] = rms_norm(act_ref[...], gain_ref[...])
        cluster = asg_ref[...]
        spread = one_hot((iota((HC * CLUSTERS, HC), 0) >> 5) == iota((HC * CLUSTERS, HC), 1))
        value = jnp.dot(spread, cluster.astype(F32).astype(BF16), preferred_element_type=F32)
        member = value == (iota((HC * CLUSTERS, TOK), 0) & (CLUSTERS - 1)).astype(F32)
        before = one_hot(iota((TOK, TOK), 0) < iota((TOK, TOK), 1))
        running = jnp.dot(one_hot(member), before, preferred_element_type=F32)
        gather = one_hot(iota((HC, HC * CLUSTERS), 0) == (iota((HC, HC * CLUSTERS), 1) >> 5))
        position = jnp.dot(
            gather, jnp.where(member, running, 0.0).astype(BF16), preferred_element_type=F32
        ).astype(jnp.int32)
        slot = slot_of(cluster, position)
        group = cluster >> 1
        row = jnp.where(
            slot < MAIN, group * MAIN + slot, GROUPS * MAIN + group * TAIL + slot - MAIN
        )
        for index in range(HC):
            rows[index] = row[index : index + 1]
        sizes[...] = jnp.dot(
            one_hot(member), jnp.ones((TOK, HD), BF16), preferred_element_type=F32
        ).astype(BF16)

    qkv = jnp.dot(normed[...], w_ref[...], preferred_element_type=F32).astype(BF16)
    which = iota((GROUPS * TAIL, CLUSTERS), 0)
    pick = one_hot(
        ((which >> 3) * 2 + (which & 7) == iota((GROUPS * TAIL, CLUSTERS), 1)) & ((which & 7) < 2)
    )
    for inner in range(HEADS_STEP):
        head = step * HEADS_STEP + inner
        table = one_hot(iota((REGION, TOK), 0) == rows[head])
        placed = jnp.dot(
            table, qkv[:, inner * 3 * HD : (inner + 1) * 3 * HD], preferred_element_type=F32
        )
        size = sizes[pl.ds(pl.multiple_of(head * CLUSTERS, CLUSTERS), CLUSTERS), :]
        tails = []
        groups = slice(inner * GROUPS, (inner + 1) * GROUPS)
        for kind in range(3):
            part = placed[:, kind * HD : (kind + 1) * HD]
            out_ref[groups, kind * MAIN : (kind + 1) * MAIN, :] = (
                part[: GROUPS * MAIN].astype(BF16).reshape(GROUPS, MAIN, HD)
            )
            tails.append(part[GROUPS * MAIN :].reshape(GROUPS, TAIL, HD))
        tails.append(jnp.dot(pick, size, preferred_element_type=F32).reshape(GROUPS, TAIL, HD))
        out_ref[groups, 3 * MAIN :, :] = jnp.concatenate(tails, axis=1).astype(BF16)


def pre_call(activations, norm_gain, w_cluster, assignment):
    return pl.pallas_call(
        pre_kernel,
        grid=(HC // HEADS_STEP,),
        in_specs=[
            pl.BlockSpec((TOK, D), lambda h: (0, 0)),
            pl.BlockSpec((1, D), lambda h: (0, 0)),
            pl.BlockSpec((D, HEADS_STEP * 3 * HD), lambda h: (0, h)),
            pl.BlockSpec((HC, TOK), lambda h: (0, 0)),
        ],
        out_specs=pl.BlockSpec((HEADS_STEP * GROUPS, PACK, HD), lambda h: (h, 0, 0)),
        out_shape=jax.ShapeDtypeStruct((SHARDS, PACK, HD), BF16),
        scratch_shapes=[
            pltpu.VMEM((TOK, D), BF16),
            pltpu.VMEM((HC, 1, TOK), jnp.int32),
            pltpu.VMEM((HC * CLUSTERS, HD), BF16),
        ],
        compiler_params=pltpu.CompilerParams(vmem_limit_bytes=VMEM),
        name="place",
    )(activations, norm_gain.reshape(1, D), w_cluster, assignment.T)


def softmax_of(scores, axis):
    highest = jnp.max(scores, axis=axis, keepdims=True)
    raised = jnp.exp2((scores - highest) * EXP2_SCALE)
    total = jnp.sum(raised, axis=axis, keepdims=True)
    return (raised * (1.0 / total)).astype(BF16)


def window_kernel(first_ref, qkv_ref, rim_ref, act_ref, w_ref, out_ref, mix):
    width = HL * HD
    step = 128
    shift = jnp.where(first_ref[0] == 0, WIN, 0)
    for head in range(HL):
        lanes = slice(head * HD, (head + 1) * HD)
        key_lanes = slice(width + head * HD, width + (head + 1) * HD)
        value_lanes = slice(2 * width + head * HD, 2 * width + (head + 1) * HD)
        for low in range(0, TOK, step):
            high = low + step
            query = qkv_ref[low:high, lanes]
            keys = jnp.concatenate([rim_ref[low:, lanes], qkv_ref[:high, key_lanes]], axis=0)
            values = jnp.concatenate(
                [rim_ref[low:, key_lanes], qkv_ref[:high, value_lanes]], axis=0
            )
            scores = lax.dot_general(query, keys, NT, preferred_element_type=F32)
            rows = iota(scores.shape, 0)
            cols = iota(scores.shape, 1)
            allowed = (cols > rows) & (cols <= rows + WIN) & (cols + low >= shift)
            weights = softmax_of(jnp.where(allowed, scores, -1e30), 1)
            mix[low:high, lanes] = jnp.dot(weights, values, preferred_element_type=F32).astype(BF16)
    out_ref[...] = act_ref[...].astype(F32) + jnp.dot(
        mix[...], w_ref[...], preferred_element_type=F32
    )


def window_call(first, local_qkv, rim, activations, w_output):
    width = HL * HD
    return pl.pallas_call(
        window_kernel,
        grid=(1,),
        in_specs=[
            pl.BlockSpec(memory_space=pltpu.SMEM),
            pl.BlockSpec((TOK, 3 * width), lambda i: (0, 0)),
            pl.BlockSpec((WIN, 2 * width), lambda i: (0, 0)),
            pl.BlockSpec((TOK, D), lambda i: (0, 0)),
            pl.BlockSpec((width, D), lambda i: (0, 0)),
        ],
        out_specs=pl.BlockSpec((TOK, D), lambda i: (0, 0)),
        out_shape=jax.ShapeDtypeStruct((TOK, D), F32),
        scratch_shapes=[pltpu.VMEM((TOK, width), BF16)],
        compiler_params=pltpu.CompilerParams(vmem_limit_bytes=VMEM),
        cost_estimate=pl.CostEstimate(flops=10**10, bytes_accessed=10**7, transcendentals=0),
        name="window",
    )(first, local_qkv, rim, activations, w_output)


def plan_moves(pool_ref, main_rows, tail_rows, first_rows):
    source = iota((SHARDS, SHARDS), 0)
    other = iota((SHARDS, SHARDS), 1)
    earlier = one_hot(other < source)
    chunk_earlier = one_hot(other < (source & ~(CHUNK - 1)))
    own_lanes = (source & (CHUNK - 1)) == (other >> 5)
    chunk_of = one_hot(iota((CHUNKS, SHARDS), 0) == (iota((CHUNKS, SHARDS), 1) >> 2))
    leader = one_hot(iota((CHUNKS, SHARDS), 0) * CHUNK == iota((CHUNKS, SHARDS), 1))
    place = iota((CHUNKS, SHARDS), 1) & (MAIN - 1)
    tail_block = pool_ref[:, PACK - 16 :, :].reshape(SHARDS * 16, HD)
    picked = iota((SHARDS, SHARDS * 16), 1) - iota((SHARDS, SHARDS * 16), 0) * 16
    starts, sizes, firsts = [], [], []
    for which in range(2):
        size = jnp.dot(
            one_hot(picked == 8 + which), tail_block, preferred_element_type=F32
        ).astype(BF16)
        start = jnp.dot(earlier, size, preferred_element_type=F32).astype(jnp.int32)
        first = jnp.dot(chunk_earlier, size, preferred_element_type=F32).astype(jnp.int32) >> 4
        local = (start - (first << 4)).astype(F32)
        starts.append(
            jnp.dot(
                chunk_of,
                jnp.where(own_lanes, local, 0.0).astype(BF16),
                preferred_element_type=F32,
            ).astype(jnp.int32)
        )
        sizes.append(
            jnp.dot(
                chunk_of,
                jnp.where(own_lanes, size.astype(F32), 0.0).astype(BF16),
                preferred_element_type=F32,
            ).astype(jnp.int32)
        )
        firsts.append(
            jnp.dot(leader, first.astype(F32).astype(BF16), preferred_element_type=F32).astype(
                jnp.int32
            )
            << 4
        )

    def moves(slot, real):
        last = POOL - 1 - slot
        target = jnp.where(
            slot < sizes[0],
            starts[0] + slot,
            jnp.where(last < sizes[1], SPAN + starts[1] + last, -1),
        )
        return jnp.where(real, target, -1)

    main_rows[...] = moves(place, place >= 0)
    for kind in range(3):
        inside = (place >= kind * TAIL) & (place < (kind + 1) * TAIL)
        tail_rows[kind] = moves(place - kind * TAIL + MAIN, inside)
    first_rows[...] = jnp.where(iota((CHUNKS, SHARDS), 1) == 0, firsts[0], firsts[1])


def cluster_kernel(
    pool_ref, out_ref, packed, mixed, scores, turned, main_rows, tail_rows, first_rows, firsts, sem
):
    plan_moves(pool_ref, main_rows, tail_rows, first_rows)
    copy = pltpu.make_async_copy(first_rows, firsts, sem)
    copy.start()
    packed[:, :, :16] = jnp.zeros((3, 2, 16, HD), BF16)
    mixed[:, CSIZE:] = jnp.zeros((2, SPAN, HD), BF16)
    copy.wait()
    row_ids = iota((2 * SPAN, SHARDS), 0)

    @pl.loop(0, CHUNKS, unroll=2)
    def _(chunk):
        here = pl.ds(chunk, 1)
        sources = pl.ds(chunk * CHUNK, CHUNK)
        main_table = one_hot(row_ids == main_rows[here, :])
        tail = pool_ref[sources, 3 * MAIN :, :].reshape(CHUNK * MAIN, HD)
        for kind in range(3):
            main = pool_ref[sources, kind * MAIN : (kind + 1) * MAIN, :].reshape(CHUNK * MAIN, HD)
            table = jnp.concatenate(
                [main_table, one_hot(row_ids == tail_rows[kind, here, :])], axis=1
            )
            moved = jnp.dot(
                table, jnp.concatenate([main, tail], axis=0), preferred_element_type=F32
            ).astype(BF16)
            for which in range(2):
                first = pl.multiple_of(firsts[chunk, which], 16)
                part = moved[which * SPAN : (which + 1) * SPAN]
                packed[kind, which, pl.ds(first, 16), :] += part[:16]
                packed[kind, which, pl.ds(pl.multiple_of(first + 16, 16), SPAN - 16), :] = part[16:]

    for which in range(2):
        for low in range(0, CSIZE, 256):
            turned[which, :, low : low + 256] = packed[2, which, low : low + 256, :].T

    blocks = CSIZE // QBLOCK

    def score(index):
        which = index // blocks
        place = pl.ds(pl.multiple_of(index % blocks * QBLOCK, QBLOCK), QBLOCK)
        return lax.dot_general(
            packed[1, which, :CSIZE, :],
            packed[0, which, place, :],
            NT,
            preferred_element_type=F32,
        )

    scores[0] = score(0)

    @pl.loop(0, 2 * blocks, step=2)
    def _(pair):
        for inner in range(2):
            index = pair + inner
            which = index // blocks
            place = pl.ds(pl.multiple_of(index % blocks * QBLOCK, QBLOCK), QBLOCK)
            scores[1 - inner] = score(jnp.minimum(index + 1, 2 * blocks - 1))
            weights = softmax_of(scores[inner], 0)
            mix = jnp.dot(turned[which], weights, preferred_element_type=F32)
            mixed[which, place, :] = mix.T.astype(BF16)

    @pl.loop(0, CHUNKS, unroll=2)
    def _(chunk):
        here = pl.ds(chunk, 1)
        table = jnp.concatenate(
            [one_hot(row_ids == main_rows[here, :]), one_hot(row_ids == tail_rows[0, here, :])],
            axis=1,
        )
        rows = jnp.concatenate(
            [
                mixed[which, pl.ds(pl.multiple_of(firsts[chunk, which], 16), SPAN), :]
                for which in range(2)
            ],
            axis=0,
        )
        spread = lax.dot_general(table, rows, TN, preferred_element_type=F32)
        main = spread[: CHUNK * MAIN].reshape(CHUNK, MAIN, HD)
        tail = spread[CHUNK * MAIN :].reshape(CHUNK, MAIN, HD)[:, :TAIL]
        out_ref[pl.ds(pl.multiple_of(chunk * CHUNK_ROWS, 16), CHUNK_ROWS), :] = (
            jnp.concatenate([main, tail], axis=1).reshape(CHUNK_ROWS, HD).astype(BF16)
        )


def cluster_call(pool):
    return pl.pallas_call(
        cluster_kernel,
        in_specs=[pl.BlockSpec(memory_space=pltpu.VMEM)],
        out_specs=pl.BlockSpec(memory_space=pltpu.VMEM),
        out_shape=jax.ShapeDtypeStruct((SHARDS * POOL, HD), BF16),
        scratch_shapes=[
            pltpu.VMEM((3, 2, CSIZE + SPAN, HD), BF16),
            pltpu.VMEM((2, CSIZE + SPAN, HD), BF16),
            pltpu.VMEM((2, CSIZE, QBLOCK), F32),
            pltpu.VMEM((2, HD, CSIZE), BF16),
            pltpu.VMEM((CHUNKS, SHARDS), jnp.int32),
            pltpu.VMEM((3, CHUNKS, SHARDS), jnp.int32),
            pltpu.VMEM((CHUNKS, SHARDS), jnp.int32),
            pltpu.SMEM((CHUNKS, SHARDS), jnp.int32),
            pltpu.SemaphoreType.DMA,
        ],
        compiler_params=pltpu.CompilerParams(vmem_limit_bytes=VMEM),
        name="cluster",
    )(pool)


def post_kernel(back_ref, slot_ref, base_ref, w_ref, out_ref, total):
    step = pl.program_id(0)

    @pl.when(step == 0)
    def _():
        total[...] = base_ref[...]

    parts = []
    for inner in range(2):
        pick = iota((TOK, HC), 1) == step * 2 + inner
        slot = jnp.sum(jnp.where(pick, slot_ref[...], 0), axis=1, keepdims=True)
        table = one_hot(iota((TOK, REGION), 1) == slot)
        rows = back_ref[inner * REGION : (inner + 1) * REGION, :]
        parts.append(jnp.dot(table, rows, preferred_element_type=F32).astype(BF16))
    mix = jnp.concatenate(parts, axis=1)
    total[...] += jnp.dot(mix, w_ref[...], preferred_element_type=F32)

    @pl.when(step == HC // 2 - 1)
    def _():
        out_ref[...] = total[...].astype(BF16)


def post_call(back, slot, base, w_output):
    return pl.pallas_call(
        post_kernel,
        grid=(HC // 2,),
        in_specs=[
            pl.BlockSpec((2 * REGION, HD), lambda h: (h, 0)),
            pl.BlockSpec((TOK, HC), lambda h: (0, 0)),
            pl.BlockSpec((TOK, D), lambda h: (0, 0)),
            pl.BlockSpec((2 * HD, D), lambda h: (h + HL // 2, 0)),
        ],
        out_specs=pl.BlockSpec((TOK, D), lambda h: (0, 0)),
        out_shape=jax.ShapeDtypeStruct((TOK, D), BF16),
        scratch_shapes=[pltpu.VMEM((TOK, D), F32)],
        compiler_params=pltpu.CompilerParams(vmem_limit_bytes=VMEM),
        name="collect",
    )(back, slot, base, w_output)


def token_slots(assignment):
    member = assignment[:, :, None] == jnp.arange(CLUSTERS, dtype=jnp.int32)
    rows = jnp.arange(TOK, dtype=jnp.int32)
    earlier = (rows[:, None] > rows[None, :]).astype(BF16)
    running = jnp.dot(
        earlier, member.astype(BF16).reshape(TOK, HC * CLUSTERS), preferred_element_type=F32
    ).reshape(TOK, HC, CLUSTERS)
    position = jnp.sum(jnp.where(member, running, 0.0), axis=2).astype(jnp.int32)
    return (assignment >> 1) * POOL + slot_of(assignment, position)


def body(activations, norm_gain, w_local, w_cluster, w_output, assignment):
    device = lax.axis_index(AXES)
    placed = pre_call(activations, norm_gain, w_cluster, assignment)
    got_pool = lax.all_to_all(placed, AXES, split_axis=0, concat_axis=0, tiled=True)

    local_qkv = jnp.dot(
        rms_norm(activations, norm_gain), w_local, preferred_element_type=F32
    ).astype(BF16)
    slot = token_slots(assignment)

    got_pool, local_kv, slot = lax.optimization_barrier(
        (got_pool, local_qkv[:, HL * HD :], slot)
    )
    rim = lax.ppermute(local_kv, AXES, [(i, i + 1) for i in range(SHARDS - 1)])
    finished = cluster_call(got_pool)
    finished, rim = lax.optimization_barrier((finished, rim))
    came_back = lax.all_to_all(
        finished.reshape(SHARDS, POOL, HD), AXES, split_axis=0, concat_axis=0, tiled=True
    )
    base = window_call(
        jnp.minimum(device, 1).astype(jnp.int32).reshape(1), local_qkv, rim, activations, w_output
    )
    return post_call(came_back.reshape(SHARDS * POOL, HD), slot, base, w_output)


def solution(mesh):
    in_specs = (P(AXES, None), P(), P(), P(), P(), P(AXES, None))
    out_specs = P(AXES, None)
    return jax.shard_map(body, mesh=mesh, in_specs=in_specs, out_specs=out_specs, check_vma=False)
```

time: 161 us -> 144 us (0.89)
  starting transfers between devices: 31.7 us -> 22 us
  Pallas kernels: 64.6 us -> 58.5 us
  waiting for transfers between devices: 48.5 us -> 51.2 us
  local copies, waits for them, and re-layouts: 7.34 us -> 5.08 us
    all_to_all x2 -> x1, starting transfers between devices: 21.7 us -> 12 us  [body(): lax.all_to_all(placed, AXES, split_axis=0, concat_axis=0, tiled=True)]
    pallas_call x1, Pallas kernels: 33.7 us -> 29.5 us  [cluster_call(): pl.pallas_call(cluster_kernel, in_specs=[pl.BlockSpec(memory_space=pltpu....]
    all_to_all x2 -> x1, waiting for transfers between devices: 37.9 us -> 40.6 us  [body(): lax.all_to_all(placed, AXES, split_axis=0, concat_axis=0, tiled=True)]
    pallas_call x1, Pallas kernels: 12.8 us -> 10.9 us  [pre_call(): pl.pallas_call(pre_kernel, grid=(HC // HEADS_STEP,), in_specs=[pl.BlockSp...]
  transfers between devices with their start and end apart: 4 -> 3, of which waited for: 2 -> 2; matrix products, arithmetic and copies ran while one was open for 8% -> 8% of each run, Pallas kernels for 36% -> 28%
where the time goes in v2:
time: 144 us
  Pallas kernels  58.5 us (41%)
  waiting for transfers between devices  51.2 us (36%)
  starting transfers between devices  22 us (15%)
  local copies, waits for them, and re-layouts  5.08 us (4%)
  other arithmetic  3.54 us (2%)
  matrix products  3.48 us (2%)
    all_to_all x1, waiting for transfers between devices, body(): lax.all_to_all(placed, AXES, split_axis=0, concat_axis=0, tiled=True)  40.6 us
    pallas_call x1, Pallas kernels, cluster_call(): pl.pallas_call(cluster_kernel, in_specs=[pl.BlockSpec(memory_space=pltpu....  29.5 us
    all_to_all x1, starting transfers between devices, body(): lax.all_to_all(placed, AXES, split_axis=0, concat_axis=0, tiled=True)  12 us
    pallas_call x1, Pallas kernels, pre_call(): pl.pallas_call(pre_kernel, grid=(HC // HEADS_STEP,), in_specs=[pl.BlockSp...  10.9 us
    pallas_call x1, Pallas kernels, window_call(): pl.pallas_call(window_kernel, grid=(1,), in_specs=[pl.BlockSpec(memory_sp...  10.8 us
    all_to_all x1, waiting for transfers between devices, body(): lax.all_to_all(finished.reshape(SHARDS, POOL, HD), AXES, split_axis=0, co...  10.6 us
    pallas_call x1, Pallas kernels, post_call(): pl.pallas_call(post_kernel, grid=(HC // 2,), in_specs=[pl.BlockSpec((2 *...  7.33 us
    all_to_all x1, starting transfers between devices, body(): lax.all_to_all(finished.reshape(SHARDS, POOL, HD), AXES, split_axis=0, co...  7.18 us
  transfers between devices with their start and end apart: 3, of which 2 were waited for; matrix products, arithmetic and copies ran while one was open for 8% of the time, Pallas kernels for 28%

profile of v2, /device:TPU:1, one launch (start us, length us, event | category | flops | bytes accessed | tf_op | source)
XLA Modules:
  0.0 143.9 jit_solution(12352932321121890800)
XLA Ops:
  0.0 0.0 copy-start
  0.0 10.9 %place.1 = bf16[128,128,128]{2,1,0:T(8,128)(2,1)} custom-call(bf16[512,1024]{1,0:T(8,128)(2,1)} %act_ref.3, f32[1,1024]{1,0:T(1,128)} %bitcast.18, bf16[1024,3072]{1,0:T(8,128)(2,1)} %w_ref.3, s32[8,512]{1,0:T(8,128)} %bitcast.16), custom_call_target="tpu_custom_call" | custom-call | tf_op jit(solution)/shard_map/place/pallas_call | solution.py:113
  10.9 12.0 %all-to-all-start = ((bf16[128,128,128]{2,1,0:T(8,128)(2,1)}), bf16[128,128,128]{2,1,0:T(8,128)(2,1)}, u32[]{:S(2)}, u32[]{:S(2)}) async-start(bf16[128,128,128]{2,1,0:T(8,128)(2,1)} %place.1), calls=%async_computation | async-start | bytes 8388608 | tf_op jit(solution)/shard_map/all_to_all | solution.py:402
  22.9 0.1 copy.19
  23.0 1.5 %fusion = f32[512]{0:T(512)S(1)} fusion(bf16[512,1024]{1,0:T(8,128)(2,1)} %act_ref.3), kind=kLoop, calls=%fused_computation.3 | loop fusion | flops 1572352 | bytes 1050624 | tf_op jit(solution)/shard_map/reduce_sum | solution.py:53
  24.6 3.1 %convolution_convert_fusion.qkv_ref = bf16[512,1536]{1,0:T(8,128)(2,1)S(1)} fusion(bf16[1024,1536]{1,0:T(8,128)(2,1)S(1)} %copy-done, bf16[512,1024]{1,0:T(8,128)(2,1)} %act_ref.3, f32[1024]{0:T(1024)S(1)} %copy-done.3, f32[512]{0:T(512)S(1)} %add_rsqrt_fusion), kind=kOutput, calls=%fused_computation | convolution fusion | flops 1613496320 | bytes 5773312 | tf_op jit(solution)/shard_map/dot_general | solution.py:404
  27.7 0.0 copy-start.1
  27.7 1.2 copy-done.1
  28.9 1.1 slice.4
  30.1 0.8 copy.22
  30.9 0.1 eq.33
  31.0 0.1 bitcast_compare_fusion
  31.1 0.4 fusion.3
  31.5 0.8 copy.20
  32.4 0.8 copy.21
  33.2 1.9 %select_add_fusion.slot_ref = s32[512,8]{1,0:T(8,128)} fusion(s32[512,8]{1,0:T(8,128)} %copy.22, s32[512,8]{1,0:T(8,128)} %copy.20, s32[512,8]{1,0:T(8,128)} %copy.21, s32[512,8]{1,0:T(8,128)S(1)} %copy.19), kind=kLoop, calls=%fused_computation.14 | loop fusion | flops 16384 | bytes 81920 | tf_op jit(solution)/shard_map/add | solution.py:396
  35.1 40.6 %all-to-all-done.pool_ref = bf16[128,128,128]{2,1,0:T(8,128)(2,1)} async-done(((bf16[128,128,128]{2,1,0:T(8,128)(2,1)}), bf16[128,128,128]{2,1,0:T(8,128)(2,1)}, u32[]{:S(2)}, u32[]{:S(2)}) %all-to-all-start) | async-done | bytes 4194336 | tf_op jit(solution)/shard_map/all_to_all | solution.py:402
  75.7 2.8 %collective-permute-start = (bf16[512,1024]{1,0:T(8,128)(2,1)}, bf16[512,1024]{1,0:T(8,128)(2,1)}, u32[]{:S(2)}, u32[]{:S(2)}) collective-permute-start(bf16[512,1024]{1,0:T(8,128)(2,1)} %slice.4), channel_id=1, source_target_pairs={{0,1},{1,2},{2,3},{3,4},{4,5},{5,6},{6,7},{7,8},{8,9},{9,10},{10,1... | collective-permute-start | bytes 3145736 | tf_op jit(solution)/shard_map/ppermute | solution.py:412
  78.5 29.5 %cluster.1 = bf16[5120,128]{1,0:T(8,128)(2,1)} custom-call(bf16[128,128,128]{2,1,0:T(8,128)(2,1)} %all-to-all-done.pool_ref), custom_call_target="tpu_custom_call" | custom-call | tf_op jit(solution)/shard_map/cluster/pallas_call | solution.py:327
  108.1 0.0 collective-permute-done.rim_ref
  108.1 7.2 %all-to-all-start.1 = ((bf16[128,40,128]{2,1,0:T(8,128)(2,1)}), bf16[128,40,128]{2,1,0:T(8,128)(2,1)}, u32[]{:S(2)}, u32[]{:S(2)}) async-start(bf16[128,40,128]{2,1,0:T(8,128)(2,1)} %bitcast.15), calls=%async_computation.1 | async-start | bytes 2621440 | tf_op jit(solution)/shard_map/all_to_all | solution.py:415
  115.3 10.8 %window.1.base_ref = f32[512,1024]{1,0:T(8,128)} custom-call(s32[1]{0:T(128)} %bitcast.8.first_ref, bf16[512,1536]{1,0:T(8,128)(2,1)} %copy-done.1, bf16[512,1024]{1,0:T(8,128)(2,1)} %collective-permute-done.rim_ref, bf16[512,1024]{1,0:T(8,128)(2,1)} %act_ref.3, bf16[1536,1024]{1,0:T(8,128)(2,1)} %w_ref.5), custom_call_target="tpu_custom_call" | custom-call | flops 10000000000 | bytes 10000000 | tf_op jit(solution)/shard_map/window/pallas_call | solution.py:169
  126.0 10.6 %all-to-all-done.1 = bf16[128,40,128]{2,1,0:T(8,128)(2,1)} async-done(((bf16[128,40,128]{2,1,0:T(8,128)(2,1)}), bf16[128,40,128]{2,1,0:T(8,128)(2,1)}, u32[]{:S(2)}, u32[]{:S(2)}) %all-to-all-start.1) | async-done | bytes 1310752 | tf_op jit(solution)/shard_map/all_to_all | solution.py:415
  136.6 7.3 %collect.1 = bf16[512,1024]{1,0:T(8,128)(2,1)} custom-call(bf16[5120,128]{1,0:T(8,128)(2,1)} %bitcast.7.back_ref, s32[512,8]{1,0:T(8,128)} %select_add_fusion.slot_ref, f32[512,1024]{1,0:T(8,128)} %window.1.base_ref, bf16[1536,1024]{1,0:T(8,128)(2,1)} %w_ref.5), custom_call_target="tpu_custom_call" | custom-call | tf_op jit(solution)/shard_map/collect/pallas_call | solution.py:371
  (10 shorter events, 0.0 us)
Async XLA Ops:
  0.0 24.5 %copy-start = (bf16[1024,1536]{1,0:T(8,128)(2,1)S(1)}, bf16[1024,1536]{1,0:T(8,128)(2,1)}, u32[]{:S(2)}) copy-start(bf16[1024,1536]{1,0:T(8,128)(2,1)} %param.8) | copy-start | bytes 9437188
  10.9 12.0 %copy-start.2 = (s32[512,8]{0,1:T(8,128)S(1)}, s32[512,8]{0,1:T(8,128)}, u32[]{:S(2)}) copy-start(s32[512,8]{0,1:T(8,128)} %param.11) | copy-start | bytes 49156
  10.9 13.6 %copy-start.3 = (f32[1024]{0:T(1024)S(1)}, f32[1024]{0:T(1024)}, u32[]{:S(2)}) copy-start(f32[1024]{0:T(1024)} %param.7) | copy-start | bytes 12292
  10.9 64.8 %all-to-all-start = ((bf16[128,128,128]{2,1,0:T(8,128)(2,1)}), bf16[128,128,128]{2,1,0:T(8,128)(2,1)}, u32[]{:S(2)}, u32[]{:S(2)}) async-start(bf16[128,128,128]{2,1,0:T(8,128)(2,1)} %place.1), calls=%async_computation | async-start | bytes 8388608 | tf_op jit(solution)/shard_map/all_to_all | solution.py:402
  27.7 1.2 copy-start.1
  75.7 32.4 %collective-permute-start = (bf16[512,1024]{1,0:T(8,128)(2,1)}, bf16[512,1024]{1,0:T(8,128)(2,1)}, u32[]{:S(2)}, u32[]{:S(2)}) collective-permute-start(bf16[512,1024]{1,0:T(8,128)(2,1)} %slice.4), channel_id=1, source_target_pairs={{0,1},{1,2},{2,3},{3,4},{4,5},{5,6},{6,7},{7,8},{8,9},{9,10},{10,1... | collective-permute-start | bytes 3145736 | tf_op jit(solution)/shard_map/ppermute | solution.py:412
  108.1 28.6 %all-to-all-start.1 = ((bf16[128,40,128]{2,1,0:T(8,128)(2,1)}), bf16[128,40,128]{2,1,0:T(8,128)(2,1)}, u32[]{:S(2)}, u32[]{:S(2)}) async-start(bf16[128,40,128]{2,1,0:T(8,128)(2,1)} %bitcast.15), calls=%async_computation.1 | async-start | bytes 2621440 | tf_op jit(solution)/shard_map/all_to_all | solution.py:415

commit v3 on v2

--- a/solution.py
+++ b/solution.py
@@ -30,6 +30,7 @@
 CHUNK_ROWS = CHUNK * POOL
 SPAN = CHUNK * PER_CLUSTER + 16
 QBLOCK = 512
+PARTS = 4
 EPSILON = 1e-06
 AXES = ("sx", "sy")
 VMEM = 60 * 2**20
@@ -185,7 +186,7 @@
     )(first, local_qkv, rim, activations, w_output)
 
 
-def plan_moves(pool_ref, main_rows, tail_rows, first_rows):
+def plan_moves(meta, main_rows, tail_rows, back_rows, first_rows):
     source = iota((SHARDS, SHARDS), 0)
     other = iota((SHARDS, SHARDS), 1)
     earlier = one_hot(other < source)
@@ -194,7 +195,7 @@
     chunk_of = one_hot(iota((CHUNKS, SHARDS), 0) == (iota((CHUNKS, SHARDS), 1) >> 2))
     leader = one_hot(iota((CHUNKS, SHARDS), 0) * CHUNK == iota((CHUNKS, SHARDS), 1))
     place = iota((CHUNKS, SHARDS), 1) & (MAIN - 1)
-    tail_block = pool_ref[:, PACK - 16 :, :].reshape(SHARDS * 16, HD)
+    tail_block = meta[...].reshape(SHARDS * 16, HD)
     picked = iota((SHARDS, SHARDS * 16), 1) - iota((SHARDS, SHARDS * 16), 0) * 16
     starts, sizes, firsts = [], [], []
     for which in range(2):
@@ -234,32 +235,68 @@
         )
         return jnp.where(real, target, -1)
 
-    main_rows[...] = moves(place, place >= 0)
+    main = moves(place, place >= 0)
+    main_rows[...] = main
+    tails = []
     for kind in range(3):
         inside = (place >= kind * TAIL) & (place < (kind + 1) * TAIL)
-        tail_rows[kind] = moves(place - kind * TAIL + MAIN, inside)
+        tails.append(moves(place - kind * TAIL + MAIN, inside))
+        tail_rows[kind] = tails[kind]
+    back_rows[...] = (
+        jnp.concatenate(
+            [
+                main.astype(F32).T.reshape(CHUNK, MAIN, CHUNKS),
+                tails[0].astype(F32).T.reshape(CHUNK, MAIN, CHUNKS)[:, :TAIL],
+            ],
+            axis=1,
+        )
+        .reshape(CHUNK_ROWS, CHUNKS)
+        .astype(BF16)
+    )
     first_rows[...] = jnp.where(iota((CHUNKS, SHARDS), 1) == 0, firsts[0], firsts[1])
 
 
 def cluster_kernel(
-    pool_ref, out_ref, packed, mixed, scores, turned, main_rows, tail_rows, first_rows, firsts, sem
+    pool_hbm,
+    out_ref,
+    pool,
+    meta,
+    packed,
+    mixed,
+    scores,
+    turned,
+    main_rows,
+    tail_rows,
+    back_rows,
+    first_rows,
+    firsts,
+    arrived,
+    planned,
 ):
-    plan_moves(pool_ref, main_rows, tail_rows, first_rows)
-    copy = pltpu.make_async_copy(first_rows, firsts, sem)
-    copy.start()
+    part = SHARDS // PARTS
+    head_copy = pltpu.make_async_copy(pool_hbm.at[:, PACK - 16 :, :], meta, arrived.at[PARTS])
+    head_copy.start()
+    copies = []
+    for index in range(PARTS):
+        span = pl.ds(index * part, part)
+        copies.append(pltpu.make_async_copy(pool_hbm.at[span], pool.at[span], arrived.at[index]))
+        copies[index].start()
     packed[:, :, :16] = jnp.zeros((3, 2, 16, HD), BF16)
     mixed[:, CSIZE:] = jnp.zeros((2, SPAN, HD), BF16)
-    copy.wait()
+    head_copy.wait()
+    plan_moves(meta, main_rows, tail_rows, back_rows, first_rows)
+    plan_copy = pltpu.make_async_copy(first_rows, firsts, planned)
+    plan_copy.start()
+    plan_copy.wait()
     row_ids = iota((2 * SPAN, SHARDS), 0)
 
-    @pl.loop(0, CHUNKS, unroll=2)
-    def _(chunk):
+    def compact(chunk):
         here = pl.ds(chunk, 1)
         sources = pl.ds(chunk * CHUNK, CHUNK)
         main_table = one_hot(row_ids == main_rows[here, :])
-        tail = pool_ref[sources, 3 * MAIN :, :].reshape(CHUNK * MAIN, HD)
+        tail = pool[sources, 3 * MAIN :, :].reshape(CHUNK * MAIN, HD)
         for kind in range(3):
-            main = pool_ref[sources, kind * MAIN : (kind + 1) * MAIN, :].reshape(CHUNK * MAIN, HD)
+            main = pool[sources, kind * MAIN : (kind + 1) * MAIN, :].reshape(CHUNK * MAIN, HD)
             table = jnp.concatenate(
                 [main_table, one_hot(row_ids == tail_rows[kind, here, :])], axis=1
             )
@@ -268,9 +305,13 @@
             ).astype(BF16)
             for which in range(2):
                 first = pl.multiple_of(firsts[chunk, which], 16)
-                part = moved[which * SPAN : (which + 1) * SPAN]
-                packed[kind, which, pl.ds(first, 16), :] += part[:16]
-                packed[kind, which, pl.ds(pl.multiple_of(first + 16, 16), SPAN - 16), :] = part[16:]
+                rows = moved[which * SPAN : (which + 1) * SPAN]
+                packed[kind, which, pl.ds(first, 16), :] += rows[:16]
+                packed[kind, which, pl.ds(pl.multiple_of(first + 16, 16), SPAN - 16), :] = rows[16:]
+
+    for index in range(PARTS):
+        copies[index].wait()
+        pl.loop(index * CHUNKS // PARTS, (index + 1) * CHUNKS // PARTS, unroll=8)(compact)
 
     for which in range(2):
         for low in range(0, CSIZE, 256):
@@ -301,13 +342,11 @@
             mix = jnp.dot(turned[which], weights, preferred_element_type=F32)
             mixed[which, place, :] = mix.T.astype(BF16)
 
-    @pl.loop(0, CHUNKS, unroll=2)
+    @pl.loop(0, CHUNKS, unroll=8)
     def _(chunk):
-        here = pl.ds(chunk, 1)
-        table = jnp.concatenate(
-            [one_hot(row_ids == main_rows[here, :]), one_hot(row_ids == tail_rows[0, here, :])],
-            axis=1,
-        )
+        spread = one_hot(iota((CHUNKS, 2 * SPAN), 0) == chunk)
+        target = jnp.dot(back_rows[...], spread, preferred_element_type=F32)
+        table = one_hot(target == iota((CHUNK_ROWS, 2 * SPAN), 1).astype(F32))
         rows = jnp.concatenate(
             [
                 mixed[which, pl.ds(pl.multiple_of(firsts[chunk, which], 16), SPAN), :]
@@ -315,29 +354,30 @@
             ],
             axis=0,
         )
-        spread = lax.dot_general(table, rows, TN, preferred_element_type=F32)
-        main = spread[: CHUNK * MAIN].reshape(CHUNK, MAIN, HD)
-        tail = spread[CHUNK * MAIN :].reshape(CHUNK, MAIN, HD)[:, :TAIL]
-        out_ref[pl.ds(pl.multiple_of(chunk * CHUNK_ROWS, 16), CHUNK_ROWS), :] = (
-            jnp.concatenate([main, tail], axis=1).reshape(CHUNK_ROWS, HD).astype(BF16)
-        )
+        out_ref[pl.ds(pl.multiple_of(chunk * CHUNK_ROWS, 16), CHUNK_ROWS), :] = jnp.dot(
+            table, rows, preferred_element_type=F32
+        ).astype(BF16)
 
 
 def cluster_call(pool):
     return pl.pallas_call(
         cluster_kernel,
-        in_specs=[pl.BlockSpec(memory_space=pltpu.VMEM)],
+        in_specs=[pl.BlockSpec(memory_space=pl.ANY)],
         out_specs=pl.BlockSpec(memory_space=pltpu.VMEM),
         out_shape=jax.ShapeDtypeStruct((SHARDS * POOL, HD), BF16),
         scratch_shapes=[
+            pltpu.VMEM((SHARDS, PACK, HD), BF16),
+            pltpu.VMEM((SHARDS, 16, HD), BF16),
             pltpu.VMEM((3, 2, CSIZE + SPAN, HD), BF16),
             pltpu.VMEM((2, CSIZE + SPAN, HD), BF16),
             pltpu.VMEM((2, CSIZE, QBLOCK), F32),
             pltpu.VMEM((2, HD, CSIZE), BF16),
             pltpu.VMEM((CHUNKS, SHARDS), jnp.int32),
             pltpu.VMEM((3, CHUNKS, SHARDS), jnp.int32),
+            pltpu.VMEM((CHUNK_ROWS, CHUNKS), BF16),
             pltpu.VMEM((CHUNKS, SHARDS), jnp.int32),
             pltpu.SMEM((CHUNKS, SHARDS), jnp.int32),
+            pltpu.SemaphoreType.DMA((PARTS + 1,)),
             pltpu.SemaphoreType.DMA,
         ],
         compiler_params=pltpu.CompilerParams(vmem_limit_bytes=VMEM),
@@ -345,41 +385,52 @@
     )(pool)
 
 
-def post_kernel(back_ref, slot_ref, base_ref, w_ref, out_ref, total):
-    step = pl.program_id(0)
-
-    @pl.when(step == 0)
-    def _():
-        total[...] = base_ref[...]
-
-    parts = []
-    for inner in range(2):
-        pick = iota((TOK, HC), 1) == step * 2 + inner
-        slot = jnp.sum(jnp.where(pick, slot_ref[...], 0), axis=1, keepdims=True)
-        table = one_hot(iota((TOK, REGION), 1) == slot)
-        rows = back_ref[inner * REGION : (inner + 1) * REGION, :]
-        parts.append(jnp.dot(table, rows, preferred_element_type=F32).astype(BF16))
-    mix = jnp.concatenate(parts, axis=1)
-    total[...] += jnp.dot(mix, w_ref[...], preferred_element_type=F32)
-
-    @pl.when(step == HC // 2 - 1)
-    def _():
-        out_ref[...] = total[...].astype(BF16)
+def post_kernel(back_hbm, slot_ref, base_hbm, w_hbm, out_ref, back, base, weights, mix, sems):
+    copies = []
+    for index in range(HC // 2):
+        span = pl.ds(index * 2 * REGION, 2 * REGION)
+        copies.append(pltpu.make_async_copy(back_hbm.at[span], back.at[span], sems.at[index]))
+    copies.append(
+        pltpu.make_async_copy(w_hbm.at[pl.ds(HL * HD, HC * HD)], weights, sems.at[HC // 2])
+    )
+    copies.append(pltpu.make_async_copy(base_hbm, base, sems.at[HC // 2 + 1]))
+    for copy in copies:
+        copy.start()
+    columns = iota((TOK, REGION), 1)
+    for head in range(HC):
+        if head % 2 == 0:
+            copies[head // 2].wait()
+        table = one_hot(columns == slot_ref[:, head : head + 1])
+        mix[:, head * HD : (head + 1) * HD] = jnp.dot(
+            table, back[head * REGION : (head + 1) * REGION, :], preferred_element_type=F32
+        ).astype(BF16)
+    copies[-2].wait()
+    copies[-1].wait()
+    for low in range(0, TOK, 256):
+        rows = slice(low, low + 256)
+        out_ref[rows, :] = (
+            base[rows, :] + jnp.dot(mix[rows, :], weights[...], preferred_element_type=F32)
+        ).astype(BF16)
 
 
 def post_call(back, slot, base, w_output):
     return pl.pallas_call(
         post_kernel,
-        grid=(HC // 2,),
         in_specs=[
-            pl.BlockSpec((2 * REGION, HD), lambda h: (h, 0)),
-            pl.BlockSpec((TOK, HC), lambda h: (0, 0)),
-            pl.BlockSpec((TOK, D), lambda h: (0, 0)),
-            pl.BlockSpec((2 * HD, D), lambda h: (h + HL // 2, 0)),
-        ],
-        out_specs=pl.BlockSpec((TOK, D), lambda h: (0, 0)),
+            pl.BlockSpec(memory_space=pl.ANY),
+            pl.BlockSpec(memory_space=pltpu.VMEM),
+            pl.BlockSpec(memory_space=pl.ANY),
+            pl.BlockSpec(memory_space=pl.ANY),
+        ],
+        out_specs=pl.BlockSpec(memory_space=pltpu.VMEM),
         out_shape=jax.ShapeDtypeStruct((TOK, D), BF16),
-        scratch_shapes=[pltpu.VMEM((TOK, D), F32)],
+        scratch_shapes=[
+            pltpu.VMEM((HC * REGION, HD), BF16),
+            pltpu.VMEM((TOK, D), F32),
+            pltpu.VMEM((HC * HD, D), BF16),
+            pltpu.VMEM((TOK, HC * HD), BF16),
+            pltpu.SemaphoreType.DMA((HC // 2 + 2,)),
+        ],
         compiler_params=pltpu.CompilerParams(vmem_limit_bytes=VMEM),
         name="collect",
     )(back, slot, base, w_output)

time: 144 us -> 139 us (0.965)
  Pallas kernels: 58.5 us -> 53.2 us
    pallas_call x2, Pallas kernels: 36.8 us -> 31.5 us  [the longest x1 24.7 us: cluster_call(): pl.pallas_call(cluster_kernel, in_specs=[pl.BlockSpec(memory_space=pl.ANY...]
  transfers between devices with their start and end apart: 3 -> 3, of which waited for: 2 -> 2; matrix products, arithmetic and copies ran while one was open for 8% -> 8% of each run, Pallas kernels for 28% -> 26%
where the time goes in v3:
time: 139 us
  Pallas kernels  53.2 us (38%)
  waiting for transfers between devices  51.2 us (37%)
  starting transfers between devices  22.1 us (16%)
  local copies, waits for them, and re-layouts  5.08 us (4%)
  other arithmetic  3.54 us (3%)
  matrix products  3.48 us (3%)
    all_to_all x1, waiting for transfers between devices, body(): lax.all_to_all(placed, AXES, split_axis=0, concat_axis=0, tiled=True)  40.6 us
    pallas_call x1, Pallas kernels, cluster_call(): pl.pallas_call(cluster_kernel, in_specs=[pl.BlockSpec(memory_space=pl.ANY...  24.7 us
    all_to_all x1, starting transfers between devices, body(): lax.all_to_all(placed, AXES, split_axis=0, concat_axis=0, tiled=True)  12 us
    pallas_call x1, Pallas kernels, pre_call(): pl.pallas_call(pre_kernel, grid=(HC // HEADS_STEP,), in_specs=[pl.BlockSp...  10.9 us
    pallas_call x1, Pallas kernels, window_call(): pl.pallas_call(window_kernel, grid=(1,), in_specs=[pl.BlockSpec(memory_sp...  10.8 us
    all_to_all x1, waiting for transfers between devices, body(): lax.all_to_all(finished.reshape(SHARDS, POOL, HD), AXES, split_axis=0, co...  10.6 us
    all_to_all x1, starting transfers between devices, body(): lax.all_to_all(finished.reshape(SHARDS, POOL, HD), AXES, split_axis=0, co...  7.15 us
    pallas_call x1, Pallas kernels, post_call(): pl.pallas_call(post_kernel, in_specs=[pl.BlockSpec(memory_space=pl.ANY),...  6.77 us
  transfers between devices with their start and end apart: 3, of which 2 were waited for; matrix products, arithmetic and copies ran while one was open for 8% of the time, Pallas kernels for 26%

profile of v3, /device:TPU:1, one launch (start us, length us, event | category | flops | bytes accessed | tf_op | source)
XLA Modules:
  0.0 139.0 jit_solution(8472772003734059371)
XLA Ops:
  0.0 0.0 copy-start
  0.0 10.9 %place.1 = bf16[128,128,128]{2,1,0:T(8,128)(2,1)} custom-call(bf16[512,1024]{1,0:T(8,128)(2,1)} %act_ref.3, f32[1,1024]{1,0:T(1,128)} %bitcast.18, bf16[1024,3072]{1,0:T(8,128)(2,1)} %w_ref.2, s32[8,512]{1,0:T(8,128)} %bitcast.16), custom_call_target="tpu_custom_call" | custom-call | tf_op jit(solution)/shard_map/place/pallas_call | solution.py:114
  10.9 12.0 %all-to-all-start = ((bf16[128,128,128]{2,1,0:T(8,128)(2,1)}), bf16[128,128,128]{2,1,0:T(8,128)(2,1)}, u32[]{:S(2)}, u32[]{:S(2)}) async-start(bf16[128,128,128]{2,1,0:T(8,128)(2,1)} %place.1), calls=%async_computation | async-start | bytes 8388608 | tf_op jit(solution)/shard_map/all_to_all | solution.py:453
  22.9 0.0 copy-done.2
  22.9 0.1 copy.19
  23.0 1.5 %fusion = f32[512]{0:T(512)S(1)} fusion(bf16[512,1024]{1,0:T(8,128)(2,1)} %act_ref.3), kind=kLoop, calls=%fused_computation.3 | loop fusion | flops 1572352 | bytes 1050624 | tf_op jit(solution)/shard_map/reduce_sum | solution.py:54
  24.6 3.1 %convolution_convert_fusion.qkv_ref = bf16[512,1536]{1,0:T(8,128)(2,1)S(1)} fusion(bf16[1024,1536]{1,0:T(8,128)(2,1)S(1)} %copy-done, bf16[512,1024]{1,0:T(8,128)(2,1)} %act_ref.3, f32[1024]{0:T(1024)S(1)} %copy-done.3, f32[512]{0:T(512)S(1)} %add_rsqrt_fusion), kind=kOutput, calls=%fused_computation | convolution fusion | flops 1613496320 | bytes 5773312 | tf_op jit(solution)/shard_map/dot_general | solution.py:455
  27.7 1.2 copy-done.1
  28.9 1.1 slice.4
  30.1 0.8 copy.22
  30.9 0.1 eq.33
  31.0 0.1 bitcast_compare_fusion
  31.1 0.4 fusion.3
  31.5 0.8 copy.20
  32.4 0.8 copy.21
  33.2 1.9 %select_add_fusion.slot_ref = s32[512,8]{1,0:T(8,128)} fusion(s32[512,8]{1,0:T(8,128)} %copy.22, s32[512,8]{1,0:T(8,128)} %copy.20, s32[512,8]{1,0:T(8,128)} %copy.21, s32[512,8]{1,0:T(8,128)S(1)} %copy.19), kind=kLoop, calls=%fused_computation.14 | loop fusion | flops 16384 | bytes 81920 | tf_op jit(solution)/shard_map/add | solution.py:447
  35.1 40.6 %all-to-all-done.pool_hbm = bf16[128,128,128]{2,1,0:T(8,128)(2,1)} async-done(((bf16[128,128,128]{2,1,0:T(8,128)(2,1)}), bf16[128,128,128]{2,1,0:T(8,128)(2,1)}, u32[]{:S(2)}, u32[]{:S(2)}) %all-to-all-start) | async-done | bytes 4194336 | tf_op jit(solution)/shard_map/all_to_all | solution.py:453
  75.7 3.0 %collective-permute-start = (bf16[512,1024]{1,0:T(8,128)(2,1)}, bf16[512,1024]{1,0:T(8,128)(2,1)}, u32[]{:S(2)}, u32[]{:S(2)}) collective-permute-start(bf16[512,1024]{1,0:T(8,128)(2,1)} %slice.4), channel_id=1, source_target_pairs={{0,1},{1,2},{2,3},{3,4},{4,5},{5,6},{6,7},{7,8},{8,9},{9,10},{10,1... | collective-permute-start | bytes 3145736 | tf_op jit(solution)/shard_map/ppermute | solution.py:463
  78.7 24.7 %cluster.1 = bf16[5120,128]{1,0:T(8,128)(2,1)} custom-call(bf16[128,128,128]{2,1,0:T(8,128)(2,1)} %all-to-all-done.pool_hbm), custom_call_target="tpu_custom_call" | custom-call | tf_op jit(solution)/shard_map/cluster/pallas_call | solution.py:363
  103.5 0.0 collective-permute-done.rim_ref
  103.5 7.1 %all-to-all-start.1 = ((bf16[128,40,128]{2,1,0:T(8,128)(2,1)}), bf16[128,40,128]{2,1,0:T(8,128)(2,1)}, u32[]{:S(2)}, u32[]{:S(2)}) async-start(bf16[128,40,128]{2,1,0:T(8,128)(2,1)} %bitcast.15), calls=%async_computation.1 | async-start | bytes 2621440 | tf_op jit(solution)/shard_map/all_to_all | solution.py:466
  110.7 10.8 %window.1.base_hbm = f32[512,1024]{1,0:T(8,128)} custom-call(s32[1]{0:T(128)} %bitcast.8.first_ref, bf16[512,1536]{1,0:T(8,128)(2,1)} %copy-done.1, bf16[512,1024]{1,0:T(8,128)(2,1)} %collective-permute-done.rim_ref, bf16[512,1024]{1,0:T(8,128)(2,1)} %act_ref.3, bf16[1536,1024]{1,0:T(8,128)(2,1)} %w_hbm.1), custom_call_target="tpu_custom_call" | custom-call | flops 10000000000 | bytes 10000000 | tf_op jit(solution)/shard_map/window/pallas_call | solution.py:170
  121.4 10.6 %all-to-all-done.1 = bf16[128,40,128]{2,1,0:T(8,128)(2,1)} async-done(((bf16[128,40,128]{2,1,0:T(8,128)(2,1)}), bf16[128,40,128]{2,1,0:T(8,128)(2,1)}, u32[]{:S(2)}, u32[]{:S(2)}) %all-to-all-start.1) | async-done | bytes 1310752 | tf_op jit(solution)/shard_map/all_to_all | solution.py:466
  132.0 6.8 %collect.1 = bf16[512,1024]{1,0:T(8,128)(2,1)} custom-call(bf16[5120,128]{1,0:T(8,128)(2,1)} %bitcast.7.back_hbm, s32[512,8]{1,0:T(8,128)} %select_add_fusion.slot_ref, f32[512,1024]{1,0:T(8,128)} %window.1.base_hbm, bf16[1536,1024]{1,0:T(8,128)(2,1)} %w_hbm.1), custom_call_target="tpu_custom_call" | custom-call | tf_op jit(solution)/shard_map/collect/pallas_call | solution.py:417
  (10 shorter events, 0.0 us)
Async XLA Ops:
  0.0 24.5 %copy-start = (bf16[1024,1536]{1,0:T(8,128)(2,1)S(1)}, bf16[1024,1536]{1,0:T(8,128)(2,1)}, u32[]{:S(2)}) copy-start(bf16[1024,1536]{1,0:T(8,128)(2,1)} %param.8) | copy-start | bytes 9437188
  10.9 12.0 %copy-start.2 = (s32[512,8]{0,1:T(8,128)S(1)}, s32[512,8]{0,1:T(8,128)}, u32[]{:S(2)}) copy-start(s32[512,8]{0,1:T(8,128)} %param.11) | copy-start | bytes 49156
  10.9 13.6 %copy-start.3 = (f32[1024]{0:T(1024)S(1)}, f32[1024]{0:T(1024)}, u32[]{:S(2)}) copy-start(f32[1024]{0:T(1024)} %param.7) | copy-start | bytes 12292
  10.9 64.8 %all-to-all-start = ((bf16[128,128,128]{2,1,0:T(8,128)(2,1)}), bf16[128,128,128]{2,1,0:T(8,128)(2,1)}, u32[]{:S(2)}, u32[]{:S(2)}) async-start(bf16[128,128,128]{2,1,0:T(8,128)(2,1)} %place.1), calls=%async_computation | async-start | bytes 8388608 | tf_op jit(solution)/shard_map/all_to_all | solution.py:453
  27.7 1.2 copy-start.1
  75.7 27.8 %collective-permute-start = (bf16[512,1024]{1,0:T(8,128)(2,1)}, bf16[512,1024]{1,0:T(8,128)(2,1)}, u32[]{:S(2)}, u32[]{:S(2)}) collective-permute-start(bf16[512,1024]{1,0:T(8,128)(2,1)} %slice.4), channel_id=1, source_target_pairs={{0,1},{1,2},{2,3},{3,4},{4,5},{5,6},{6,7},{7,8},{8,9},{9,10},{10,1... | collective-permute-start | bytes 3145736 | tf_op jit(solution)/shard_map/ppermute | solution.py:463
  103.5 28.5 %all-to-all-start.1 = ((bf16[128,40,128]{2,1,0:T(8,128)(2,1)}), bf16[128,40,128]{2,1,0:T(8,128)(2,1)}, u32[]{:S(2)}, u32[]{:S(2)}) async-start(bf16[128,40,128]{2,1,0:T(8,128)(2,1)} %bitcast.15), calls=%async_computation.1 | async-start | bytes 2621440 | tf_op jit(solution)/shard_map/all_to_all | solution.py:466

commit v4 on v3

--- a/solution.py
+++ b/solution.py
@@ -29,7 +29,7 @@
 CHUNKS = SHARDS // CHUNK
 CHUNK_ROWS = CHUNK * POOL
 SPAN = CHUNK * PER_CLUSTER + 16
-QBLOCK = 512
+QBLOCK = 1024
 PARTS = 4
 EPSILON = 1e-06
 AXES = ("sx", "sy")
@@ -132,10 +132,10 @@
     )(activations, norm_gain.reshape(1, D), w_cluster, assignment.T)
 
 
-def softmax_of(scores, axis):
-    highest = jnp.max(scores, axis=axis, keepdims=True)
+def softmax_rows(scores):
+    highest = jnp.max(scores, axis=-1, keepdims=True)
     raised = jnp.exp2((scores - highest) * EXP2_SCALE)
-    total = jnp.sum(raised, axis=axis, keepdims=True)
+    total = jnp.sum(raised, axis=-1, keepdims=True)
     return (raised * (1.0 / total)).astype(BF16)
 
 
@@ -158,7 +158,7 @@
             rows = iota(scores.shape, 0)
             cols = iota(scores.shape, 1)
             allowed = (cols > rows) & (cols <= rows + WIN) & (cols + low >= shift)
-            weights = softmax_of(jnp.where(allowed, scores, -1e30), 1)
+            weights = softmax_rows(jnp.where(allowed, scores, -1e30))
             mix[low:high, lanes] = jnp.dot(weights, values, preferred_element_type=F32).astype(BF16)
     out_ref[...] = act_ref[...].astype(F32) + jnp.dot(
         mix[...], w_ref[...], preferred_element_type=F32
@@ -264,6 +264,7 @@
     packed,
     mixed,
     scores,
+    tops,
     turned,
     main_rows,
     tail_rows,
@@ -319,17 +320,19 @@
 
     blocks = CSIZE // QBLOCK
 
-    def score(index):
+    def score(buffer, index):
         which = index // blocks
         place = pl.ds(pl.multiple_of(index % blocks * QBLOCK, QBLOCK), QBLOCK)
-        return lax.dot_general(
+        values = lax.dot_general(
             packed[1, which, :CSIZE, :],
             packed[0, which, place, :],
             NT,
             preferred_element_type=F32,
         )
-
-    scores[0] = score(0)
+        scores[buffer] = values
+        tops[buffer] = jnp.max(values, axis=0, keepdims=True)
+
+    score(0, 0)
 
     @pl.loop(0, 2 * blocks, step=2)
     def _(pair):
@@ -337,8 +340,10 @@
             index = pair + inner
             which = index // blocks
             place = pl.ds(pl.multiple_of(index % blocks * QBLOCK, QBLOCK), QBLOCK)
-            scores[1 - inner] = score(jnp.minimum(index + 1, 2 * blocks - 1))
-            weights = softmax_of(scores[inner], 0)
+            score(1 - inner, jnp.minimum(index + 1, 2 * blocks - 1))
+            raised = jnp.exp2((scores[inner] - tops[inner]) * EXP2_SCALE)
+            scale = 1.0 / jnp.sum(raised, axis=0, keepdims=True)
+            weights = (raised * scale).astype(BF16)
             mix = jnp.dot(turned[which], weights, preferred_element_type=F32)
             mixed[which, place, :] = mix.T.astype(BF16)
 
@@ -371,6 +376,7 @@
             pltpu.VMEM((3, 2, CSIZE + SPAN, HD), BF16),
             pltpu.VMEM((2, CSIZE + SPAN, HD), BF16),
             pltpu.VMEM((2, CSIZE, QBLOCK), F32),
+            pltpu.VMEM((2, 1, QBLOCK), F32),
             pltpu.VMEM((2, HD, CSIZE), BF16),
             pltpu.VMEM((CHUNKS, SHARDS), jnp.int32),
             pltpu.VMEM((3, CHUNKS, SHARDS), jnp.int32),
@@ -457,9 +463,7 @@
     ).astype(BF16)
     slot = token_slots(assignment)
 
-    got_pool, local_kv, slot = lax.optimization_barrier(
-        (got_pool, local_qkv[:, HL * HD :], slot)
-    )
+    local_kv = local_qkv[:, HL * HD :]
     rim = lax.ppermute(local_kv, AXES, [(i, i + 1) for i in range(SHARDS - 1)])
     finished = cluster_call(got_pool)
     finished, rim = lax.optimization_barrier((finished, rim))

time: 139 us -> 133 us (0.957)
  waiting for transfers between devices: 51.2 us -> 47.9 us
    all_to_all x1, waiting for transfers between devices: 10.6 us -> 6.23 us  [body(): lax.all_to_all(finished.reshape(SHARDS, POOL, HD), AXES, split_axis=0, co...]
    all_to_all x1, starting transfers between devices: 7.15 us -> 5.32 us  [body(): lax.all_to_all(finished.reshape(SHARDS, POOL, HD), AXES, split_axis=0, co...]
where the time goes in v4:
time: 133 us
  Pallas kernels  51.9 us (39%)
  waiting for transfers between devices  47.9 us (36%)
  starting transfers between devices  20.8 us (16%)
  local copies, waits for them, and re-layouts  5.07 us (4%)
  other arithmetic  3.52 us (3%)
  matrix products  3.48 us (3%)
    all_to_all x1, waiting for transfers between devices, body(): lax.all_to_all(placed, AXES, split_axis=0, concat_axis=0, tiled=True)  41.6 us
    pallas_call x1, Pallas kernels, cluster_call(): pl.pallas_call(cluster_kernel, in_specs=[pl.BlockSpec(memory_space=pl.ANY...  23.4 us
    all_to_all x1, starting transfers between devices, body(): lax.all_to_all(placed, AXES, split_axis=0, concat_axis=0, tiled=True)  12 us
    pallas_call x1, Pallas kernels, pre_call(): pl.pallas_call(pre_kernel, grid=(HC // HEADS_STEP,), in_specs=[pl.BlockSp...  10.9 us
    pallas_call x1, Pallas kernels, window_call(): pl.pallas_call(window_kernel, grid=(1,), in_specs=[pl.BlockSpec(memory_sp...  10.8 us
    pallas_call x1, Pallas kernels, post_call(): pl.pallas_call(post_kernel, in_specs=[pl.BlockSpec(memory_space=pl.ANY),...  6.78 us
    all_to_all x1, waiting for transfers between devices, body(): lax.all_to_all(finished.reshape(SHARDS, POOL, HD), AXES, split_axis=0, co...  6.23 us
    all_to_all x1, starting transfers between devices, body(): lax.all_to_all(finished.reshape(SHARDS, POOL, HD), AXES, split_axis=0, co...  5.32 us
  transfers between devices with their start and end apart: 3, of which 2 were waited for; matrix products, arithmetic and copies ran while one was open for 8% of the time, Pallas kernels for 26%

profile of v4, /device:TPU:1, one launch (start us, length us, event | category | flops | bytes accessed | tf_op | source)
XLA Modules:
  0.0 132.9 jit_solution(9606107326844219610)
XLA Ops:
  0.0 0.0 copy-start
  0.0 10.9 %place.1 = bf16[128,128,128]{2,1,0:T(8,128)(2,1)} custom-call(bf16[512,1024]{1,0:T(8,128)(2,1)} %act_ref.3, f32[1,1024]{1,0:T(1,128)} %bitcast.18, bf16[1024,3072]{1,0:T(8,128)(2,1)} %w_ref.2, s32[8,512]{1,0:T(8,128)} %bitcast.16), custom_call_target="tpu_custom_call" | custom-call | tf_op jit(solution)/shard_map/place/pallas_call | solution.py:114
  10.9 12.0 %all-to-all-start = ((bf16[128,128,128]{2,1,0:T(8,128)(2,1)}), bf16[128,128,128]{2,1,0:T(8,128)(2,1)}, u32[]{:S(2)}, u32[]{:S(2)}) async-start(bf16[128,128,128]{2,1,0:T(8,128)(2,1)} %place.1), calls=%async_computation | async-start | bytes 8388608 | tf_op jit(solution)/shard_map/all_to_all | solution.py:459
  22.9 1.5 %fusion = f32[512]{0:T(512)S(1)} fusion(bf16[512,1024]{1,0:T(8,128)(2,1)} %act_ref.3), kind=kLoop, calls=%fused_computation.3 | loop fusion | flops 1572352 | bytes 1050624 | tf_op jit(solution)/shard_map/reduce_sum | solution.py:54
  24.4 0.0 copy-done
  24.4 3.1 %convolution_convert_fusion.qkv_ref = bf16[512,1536]{1,0:T(8,128)(2,1)S(1)} fusion(bf16[1024,1536]{1,0:T(8,128)(2,1)S(1)} %copy-done, bf16[512,1024]{1,0:T(8,128)(2,1)} %act_ref.3, f32[1024]{0:T(1024)S(1)} %copy-done.3, f32[512]{0:T(512)S(1)} %add_rsqrt_fusion), kind=kOutput, calls=%fused_computation | convolution fusion | flops 1613496320 | bytes 5773312 | tf_op jit(solution)/shard_map/dot_general | solution.py:461
  27.6 1.2 copy-done.1
  28.8 1.1 slice.4
  29.9 3.5 %collective-permute-start = (bf16[512,1024]{1,0:T(8,128)(2,1)}, bf16[512,1024]{1,0:T(8,128)(2,1)}, u32[]{:S(2)}, u32[]{:S(2)}) collective-permute-start(bf16[512,1024]{1,0:T(8,128)(2,1)} %slice.4), channel_id=1, source_target_pairs={{0,1},{1,2},{2,3},{3,4},{4,5},{5,6},{6,7},{7,8},{8,9},{9,10},{10,1... | collective-permute-start | bytes 3145736 | tf_op jit(solution)/shard_map/ppermute | solution.py:467
  33.5 0.1 eq.33
  33.5 0.1 bitcast_compare_fusion
  33.7 0.4 fusion.3
  34.1 41.6 %all-to-all-done.pool_hbm = bf16[128,128,128]{2,1,0:T(8,128)(2,1)} async-done(((bf16[128,128,128]{2,1,0:T(8,128)(2,1)}), bf16[128,128,128]{2,1,0:T(8,128)(2,1)}, u32[]{:S(2)}, u32[]{:S(2)}) %all-to-all-start) | async-done | bytes 4194336 | tf_op jit(solution)/shard_map/all_to_all | solution.py:459
  75.7 23.4 %cluster.1 = bf16[5120,128]{1,0:T(8,128)(2,1)} custom-call(bf16[128,128,128]{2,1,0:T(8,128)(2,1)} %all-to-all-done.pool_hbm), custom_call_target="tpu_custom_call" | custom-call | tf_op jit(solution)/shard_map/cluster/pallas_call | solution.py:368
  99.1 0.0 collective-permute-done.rim_ref
  99.1 5.3 %all-to-all-start.1 = ((bf16[128,40,128]{2,1,0:T(8,128)(2,1)}), bf16[128,40,128]{2,1,0:T(8,128)(2,1)}, u32[]{:S(2)}, u32[]{:S(2)}) async-start(bf16[128,40,128]{2,1,0:T(8,128)(2,1)} %bitcast.15), calls=%async_computation.1 | async-start | bytes 2621440 | tf_op jit(solution)/shard_map/all_to_all | solution.py:470
  104.5 0.1 copy.19
  104.6 0.8 copy.22
  105.5 0.8 copy.20
  106.3 0.8 copy.21
  107.1 1.8 %select_add_fusion.slot_ref = s32[512,8]{1,0:T(8,128)} fusion(s32[512,8]{1,0:T(8,128)} %copy.22, s32[512,8]{1,0:T(8,128)} %copy.20, s32[512,8]{1,0:T(8,128)} %copy.21, s32[512,8]{1,0:T(8,128)S(1)} %copy.19), kind=kLoop, calls=%fused_computation.14 | loop fusion | flops 16384 | bytes 81920 | tf_op jit(solution)/shard_map/add | solution.py:453
  109.0 10.8 %window.1.base_hbm = f32[512,1024]{1,0:T(8,128)} custom-call(s32[1]{0:T(128)} %bitcast.8.first_ref, bf16[512,1536]{1,0:T(8,128)(2,1)} %copy-done.1, bf16[512,1024]{1,0:T(8,128)(2,1)} %collective-permute-done.rim_ref, bf16[512,1024]{1,0:T(8,128)(2,1)} %act_ref.3, bf16[1536,1024]{1,0:T(8,128)(2,1)} %w_hbm.1), custom_call_target="tpu_custom_call" | custom-call | flops 10000000000 | bytes 10000000 | tf_op jit(solution)/shard_map/window/pallas_call | solution.py:170
  119.8 6.2 %all-to-all-done.1 = bf16[128,40,128]{2,1,0:T(8,128)(2,1)} async-done(((bf16[128,40,128]{2,1,0:T(8,128)(2,1)}), bf16[128,40,128]{2,1,0:T(8,128)(2,1)}, u32[]{:S(2)}, u32[]{:S(2)}) %all-to-all-start.1) | async-done | bytes 1310752 | tf_op jit(solution)/shard_map/all_to_all | solution.py:470
  126.0 6.8 %collect.1 = bf16[512,1024]{1,0:T(8,128)(2,1)} custom-call(bf16[5120,128]{1,0:T(8,128)(2,1)} %bitcast.3.back_hbm, s32[512,8]{1,0:T(8,128)} %select_add_fusion.slot_ref, f32[512,1024]{1,0:T(8,128)} %window.1.base_hbm, bf16[1536,1024]{1,0:T(8,128)(2,1)} %w_hbm.1), custom_call_target="tpu_custom_call" | custom-call | tf_op jit(solution)/shard_map/collect/pallas_call | solution.py:423
  (10 shorter events, 0.0 us)
Async XLA Ops:
  0.0 24.4 %copy-start = (bf16[1024,1536]{1,0:T(8,128)(2,1)S(1)}, bf16[1024,1536]{1,0:T(8,128)(2,1)}, u32[]{:S(2)}) copy-start(bf16[1024,1536]{1,0:T(8,128)(2,1)} %param.8) | copy-start | bytes 9437188
  10.9 13.5 %copy-start.3 = (f32[1024]{0:T(1024)S(1)}, f32[1024]{0:T(1024)}, u32[]{:S(2)}) copy-start(f32[1024]{0:T(1024)} %param.7) | copy-start | bytes 12292
  10.9 64.8 %all-to-all-start = ((bf16[128,128,128]{2,1,0:T(8,128)(2,1)}), bf16[128,128,128]{2,1,0:T(8,128)(2,1)}, u32[]{:S(2)}, u32[]{:S(2)}) async-start(bf16[128,128,128]{2,1,0:T(8,128)(2,1)} %place.1), calls=%async_computation | async-start | bytes 8388608 | tf_op jit(solution)/shard_map/all_to_all | solution.py:459
  27.5 1.2 copy-start.1
  28.8 4.8 %copy-start.2 = (s32[512,8]{0,1:T(8,128)S(1)}, s32[512,8]{0,1:T(8,128)}, u32[]{:S(2)}) copy-start(s32[512,8]{0,1:T(8,128)} %param.11) | copy-start | bytes 49156
  29.9 69.2 %collective-permute-start = (bf16[512,1024]{1,0:T(8,128)(2,1)}, bf16[512,1024]{1,0:T(8,128)(2,1)}, u32[]{:S(2)}, u32[]{:S(2)}) collective-permute-start(bf16[512,1024]{1,0:T(8,128)(2,1)} %slice.4), channel_id=1, source_target_pairs={{0,1},{1,2},{2,3},{3,4},{4,5},{5,6},{6,7},{7,8},{8,9},{9,10},{10,1... | collective-permute-start | bytes 3145736 | tf_op jit(solution)/shard_map/ppermute | solution.py:467
  99.1 26.8 %all-to-all-start.1 = ((bf16[128,40,128]{2,1,0:T(8,128)(2,1)}), bf16[128,40,128]{2,1,0:T(8,128)(2,1)}, u32[]{:S(2)}, u32[]{:S(2)}) async-start(bf16[128,40,128]{2,1,0:T(8,128)(2,1)} %bitcast.15), calls=%async_computation.1 | async-start | bytes 2621440 | tf_op jit(solution)/shard_map/all_to_all | solution.py:470

commit v5 on v4

--- a/solution.py
+++ b/solution.py
@@ -59,73 +59,103 @@
     return jnp.where((cluster & 1) == 1, POOL - 1 - position, position)
 
 
-def pre_kernel(act_ref, gain_ref, w_ref, asg_ref, out_ref, normed, rows, sizes):
-    step = pl.program_id(0)
-
-    @pl.when(step == 0)
-    def _():
-        normed[...] = rms_norm(act_ref[...], gain_ref[...])
-        cluster = asg_ref[...]
-        spread = one_hot((iota((HC * CLUSTERS, HC), 0) >> 5) == iota((HC * CLUSTERS, HC), 1))
-        value = jnp.dot(spread, cluster.astype(F32).astype(BF16), preferred_element_type=F32)
-        member = value == (iota((HC * CLUSTERS, TOK), 0) & (CLUSTERS - 1)).astype(F32)
-        before = one_hot(iota((TOK, TOK), 0) < iota((TOK, TOK), 1))
-        running = jnp.dot(one_hot(member), before, preferred_element_type=F32)
-        gather = one_hot(iota((HC, HC * CLUSTERS), 0) == (iota((HC, HC * CLUSTERS), 1) >> 5))
-        position = jnp.dot(
-            gather, jnp.where(member, running, 0.0).astype(BF16), preferred_element_type=F32
-        ).astype(jnp.int32)
-        slot = slot_of(cluster, position)
-        group = cluster >> 1
-        row = jnp.where(
-            slot < MAIN, group * MAIN + slot, GROUPS * MAIN + group * TAIL + slot - MAIN
+def pre_kernel(
+    act_hbm, gain_ref, w_hbm, asg_ref, out_hbm, act, weights, normed, rows, sizes, stage, arrived, leaving
+):
+    steps = HC // HEADS_STEP
+    width = HEADS_STEP * 3 * HD
+    copies = [
+        pltpu.make_async_copy(
+            w_hbm.at[:, pl.ds(step * width, width)], weights.at[step], arrived.at[step]
         )
-        for index in range(HC):
-            rows[index] = row[index : index + 1]
-        sizes[...] = jnp.dot(
-            one_hot(member), jnp.ones((TOK, HD), BF16), preferred_element_type=F32
-        ).astype(BF16)
-
-    qkv = jnp.dot(normed[...], w_ref[...], preferred_element_type=F32).astype(BF16)
+        for step in range(steps)
+    ]
+    act_copy = pltpu.make_async_copy(act_hbm, act, arrived.at[steps])
+    act_copy.start()
+    for copy in copies:
+        copy.start()
+
+    cluster = asg_ref[...]
+    spread = one_hot((iota((HC * CLUSTERS, HC), 0) >> 5) == iota((HC * CLUSTERS, HC), 1))
+    value = jnp.dot(spread, cluster.astype(F32).astype(BF16), preferred_element_type=F32)
+    member = value == (iota((HC * CLUSTERS, TOK), 0) & (CLUSTERS - 1)).astype(F32)
+    before = one_hot(iota((TOK, TOK), 0) < iota((TOK, TOK), 1))
+    running = jnp.dot(one_hot(member), before, preferred_element_type=F32)
+    gather = one_hot(iota((HC, HC * CLUSTERS), 0) == (iota((HC, HC * CLUSTERS), 1) >> 5))
+    position = jnp.dot(
+        gather, jnp.where(member, running, 0.0).astype(BF16), preferred_element_type=F32
+    ).astype(jnp.int32)
+    slot = slot_of(cluster, position)
+    group = cluster >> 1
+    rows[...] = jnp.where(
+        slot < MAIN, group * MAIN + slot, GROUPS * MAIN + group * TAIL + slot - MAIN
+    )
+    sizes[...] = jnp.dot(
+        one_hot(member), jnp.ones((TOK, HD), BF16), preferred_element_type=F32
+    ).astype(BF16)
     which = iota((GROUPS * TAIL, CLUSTERS), 0)
     pick = one_hot(
         ((which >> 3) * 2 + (which & 7) == iota((GROUPS * TAIL, CLUSTERS), 1)) & ((which & 7) < 2)
     )
-    for inner in range(HEADS_STEP):
-        head = step * HEADS_STEP + inner
-        table = one_hot(iota((REGION, TOK), 0) == rows[head])
-        placed = jnp.dot(
-            table, qkv[:, inner * 3 * HD : (inner + 1) * 3 * HD], preferred_element_type=F32
-        )
-        size = sizes[pl.ds(pl.multiple_of(head * CLUSTERS, CLUSTERS), CLUSTERS), :]
-        tails = []
-        groups = slice(inner * GROUPS, (inner + 1) * GROUPS)
-        for kind in range(3):
-            part = placed[:, kind * HD : (kind + 1) * HD]
-            out_ref[groups, kind * MAIN : (kind + 1) * MAIN, :] = (
-                part[: GROUPS * MAIN].astype(BF16).reshape(GROUPS, MAIN, HD)
+    act_copy.wait()
+    normed[...] = rms_norm(act[...], gain_ref[...])
+
+    def project(step):
+        copies[step].wait()
+        return jnp.dot(normed[...], weights[step], preferred_element_type=F32).astype(BF16)
+
+    sent = []
+    qkv = project(0)
+    for step in range(steps):
+        later = project(step + 1) if step + 1 < steps else None
+        for inner in range(HEADS_STEP):
+            head = step * HEADS_STEP + inner
+            table = one_hot(iota((REGION, TOK), 0) == rows[head : head + 1, :])
+            placed = jnp.dot(
+                table, qkv[:, inner * 3 * HD : (inner + 1) * 3 * HD], preferred_element_type=F32
             )
-            tails.append(part[GROUPS * MAIN :].reshape(GROUPS, TAIL, HD))
-        tails.append(jnp.dot(pick, size, preferred_element_type=F32).reshape(GROUPS, TAIL, HD))
-        out_ref[groups, 3 * MAIN :, :] = jnp.concatenate(tails, axis=1).astype(BF16)
+            groups = slice(head * GROUPS, (head + 1) * GROUPS)
+            tails = []
+            for kind in range(3):
+                part = placed[:, kind * HD : (kind + 1) * HD]
+                stage[groups, kind * MAIN : (kind + 1) * MAIN, :] = (
+                    part[: GROUPS * MAIN].astype(BF16).reshape(GROUPS, MAIN, HD)
+                )
+                tails.append(part[GROUPS * MAIN :].reshape(GROUPS, TAIL, HD))
+            size = sizes[head * CLUSTERS : (head + 1) * CLUSTERS, :]
+            tails.append(
+                jnp.dot(pick, size, preferred_element_type=F32).reshape(GROUPS, TAIL, HD)
+            )
+            stage[groups, 3 * MAIN :, :] = jnp.concatenate(tails, axis=1).astype(BF16)
+        span = pl.ds(step * HEADS_STEP * GROUPS, HEADS_STEP * GROUPS)
+        sent.append(pltpu.make_async_copy(stage.at[span], out_hbm.at[span], leaving.at[step]))
+        sent[step].start()
+        qkv = later
+    for copy in sent:
+        copy.wait()
 
 
 def pre_call(activations, norm_gain, w_cluster, assignment):
+    steps = HC // HEADS_STEP
     return pl.pallas_call(
         pre_kernel,
-        grid=(HC // HEADS_STEP,),
         in_specs=[
-            pl.BlockSpec((TOK, D), lambda h: (0, 0)),
-            pl.BlockSpec((1, D), lambda h: (0, 0)),
-            pl.BlockSpec((D, HEADS_STEP * 3 * HD), lambda h: (0, h)),
-            pl.BlockSpec((HC, TOK), lambda h: (0, 0)),
+            pl.BlockSpec(memory_space=pl.ANY),
+            pl.BlockSpec(memory_space=pltpu.VMEM),
+            pl.BlockSpec(memory_space=pl.ANY),
+            pl.BlockSpec(memory_space=pltpu.VMEM),
         ],
-        out_specs=pl.BlockSpec((HEADS_STEP * GROUPS, PACK, HD), lambda h: (h, 0, 0)),
+        out_specs=pl.BlockSpec(memory_space=pl.ANY),
         out_shape=jax.ShapeDtypeStruct((SHARDS, PACK, HD), BF16),
         scratch_shapes=[
             pltpu.VMEM((TOK, D), BF16),
-            pltpu.VMEM((HC, 1, TOK), jnp.int32),
+            pltpu.VMEM((steps, D, HEADS_STEP * 3 * HD), BF16),
+            pltpu.VMEM((TOK, D), BF16),
+            pltpu.VMEM((HC, TOK), jnp.int32),
             pltpu.VMEM((HC * CLUSTERS, HD), BF16),
+            pltpu.VMEM((SHARDS, PACK, HD), BF16),
+            pltpu.SemaphoreType.DMA((steps + 1,)),
+            pltpu.SemaphoreType.DMA((steps,)),
         ],
         compiler_params=pltpu.CompilerParams(vmem_limit_bytes=VMEM),
         name="place",
@@ -191,12 +221,18 @@
     other = iota((SHARDS, SHARDS), 1)
     earlier = one_hot(other < source)
     chunk_earlier = one_hot(other < (source & ~(CHUNK - 1)))
-    own_lanes = (source & (CHUNK - 1)) == (other >> 5)
+    own_lanes = [(source & (CHUNK - 1)) == (other >> shift) for shift in (5, 3)]
     chunk_of = one_hot(iota((CHUNKS, SHARDS), 0) == (iota((CHUNKS, SHARDS), 1) >> 2))
     leader = one_hot(iota((CHUNKS, SHARDS), 0) * CHUNK == iota((CHUNKS, SHARDS), 1))
-    place = iota((CHUNKS, SHARDS), 1) & (MAIN - 1)
+    lane = iota((CHUNKS, SHARDS), 1)
     tail_block = meta[...].reshape(SHARDS * 16, HD)
     picked = iota((SHARDS, SHARDS * 16), 1) - iota((SHARDS, SHARDS * 16), 0) * 16
+
+    def by_chunk(values, own):
+        return jnp.dot(
+            chunk_of, jnp.where(own, values, 0.0).astype(BF16), preferred_element_type=F32
+        ).astype(jnp.int32)
+
     starts, sizes, firsts = [], [], []
     for which in range(2):
         size = jnp.dot(
@@ -205,20 +241,8 @@
         start = jnp.dot(earlier, size, preferred_element_type=F32).astype(jnp.int32)
         first = jnp.dot(chunk_earlier, size, preferred_element_type=F32).astype(jnp.int32) >> 4
         local = (start - (first << 4)).astype(F32)
-        starts.append(
-            jnp.dot(
-                chunk_of,
-                jnp.where(own_lanes, local, 0.0).astype(BF16),
-                preferred_element_type=F32,
-            ).astype(jnp.int32)
-        )
-        sizes.append(
-            jnp.dot(
-                chunk_of,
-                jnp.where(own_lanes, size.astype(F32), 0.0).astype(BF16),
-                preferred_element_type=F32,
-            ).astype(jnp.int32)
-        )
+        starts.append([by_chunk(local, own) for own in own_lanes])
+        sizes.append([by_chunk(size.astype(F32), own) for own in own_lanes])
         firsts.append(
             jnp.dot(leader, first.astype(F32).astype(BF16), preferred_element_type=F32).astype(
                 jnp.int32
@@ -226,27 +250,23 @@
             << 4
         )
 
-    def moves(slot, real):
+    def moves(slot, table):
         last = POOL - 1 - slot
-        target = jnp.where(
-            slot < sizes[0],
-            starts[0] + slot,
-            jnp.where(last < sizes[1], SPAN + starts[1] + last, -1),
+        return jnp.where(
+            slot < sizes[0][table],
+            starts[0][table] + slot,
+            jnp.where(last < sizes[1][table], SPAN + starts[1][table] + last, -1),
         )
-        return jnp.where(real, target, -1)
-
-    main = moves(place, place >= 0)
+
+    main = moves(lane & (MAIN - 1), 0)
+    tail = moves(MAIN + (lane & (TAIL - 1)), 1)
     main_rows[...] = main
-    tails = []
-    for kind in range(3):
-        inside = (place >= kind * TAIL) & (place < (kind + 1) * TAIL)
-        tails.append(moves(place - kind * TAIL + MAIN, inside))
-        tail_rows[kind] = tails[kind]
+    tail_rows[...] = tail
     back_rows[...] = (
         jnp.concatenate(
             [
                 main.astype(F32).T.reshape(CHUNK, MAIN, CHUNKS),
-                tails[0].astype(F32).T.reshape(CHUNK, MAIN, CHUNKS)[:, :TAIL],
+                tail.astype(F32).T[: CHUNK * TAIL].reshape(CHUNK, TAIL, CHUNKS),
             ],
             axis=1,
         )
@@ -258,7 +278,7 @@
 
 def cluster_kernel(
     pool_hbm,
-    out_ref,
+    out_hbm,
     pool,
     meta,
     packed,
@@ -273,6 +293,8 @@
     firsts,
     arrived,
     planned,
+    result,
+    leaving,
 ):
     part = SHARDS // PARTS
     head_copy = pltpu.make_async_copy(pool_hbm.at[:, PACK - 16 :, :], meta, arrived.at[PARTS])
@@ -294,21 +316,29 @@
     def compact(chunk):
         here = pl.ds(chunk, 1)
         sources = pl.ds(chunk * CHUNK, CHUNK)
-        main_table = one_hot(row_ids == main_rows[here, :])
-        tail = pool[sources, 3 * MAIN :, :].reshape(CHUNK * MAIN, HD)
+        table = jnp.concatenate(
+            [
+                one_hot(row_ids == main_rows[here, :]),
+                one_hot(row_ids == tail_rows[here, :])[:, : CHUNK * TAIL],
+            ],
+            axis=1,
+        )
+        tail = pool[sources, 3 * MAIN :, :].astype(F32)
+        kinds = []
         for kind in range(3):
-            main = pool[sources, kind * MAIN : (kind + 1) * MAIN, :].reshape(CHUNK * MAIN, HD)
-            table = jnp.concatenate(
-                [main_table, one_hot(row_ids == tail_rows[kind, here, :])], axis=1
-            )
-            moved = jnp.dot(
-                table, jnp.concatenate([main, tail], axis=0), preferred_element_type=F32
-            ).astype(BF16)
-            for which in range(2):
-                first = pl.multiple_of(firsts[chunk, which], 16)
-                rows = moved[which * SPAN : (which + 1) * SPAN]
+            rows = pool[sources, kind * MAIN : (kind + 1) * MAIN, :].reshape(CHUNK * MAIN, HD)
+            more = tail[:, kind * TAIL : (kind + 1) * TAIL].reshape(CHUNK * TAIL, HD)
+            kinds.append(jnp.concatenate([rows, more.astype(BF16)], axis=0))
+        moved = jnp.dot(
+            table, jnp.concatenate(kinds, axis=1), preferred_element_type=F32
+        ).astype(BF16)
+        for which in range(2):
+            first = pl.multiple_of(firsts[chunk, which], 16)
+            rest = pl.ds(pl.multiple_of(first + 16, 16), SPAN - 16)
+            for kind in range(3):
+                rows = moved[which * SPAN : (which + 1) * SPAN, kind * HD : (kind + 1) * HD]
                 packed[kind, which, pl.ds(first, 16), :] += rows[:16]
-                packed[kind, which, pl.ds(pl.multiple_of(first + 16, 16), SPAN - 16), :] = rows[16:]
+                packed[kind, which, rest, :] = rows[16:]
 
     for index in range(PARTS):
         copies[index].wait()
@@ -347,28 +377,38 @@
             mix = jnp.dot(turned[which], weights, preferred_element_type=F32)
             mixed[which, place, :] = mix.T.astype(BF16)
 
-    @pl.loop(0, CHUNKS, unroll=8)
-    def _(chunk):
-        spread = one_hot(iota((CHUNKS, 2 * SPAN), 0) == chunk)
+    columns = iota((CHUNK_ROWS, 2 * SPAN), 1).astype(F32)
+    group = CHUNKS // PARTS
+    sent = []
+    for index in range(PARTS):
+        lanes = iota((CHUNKS, group * 2 * SPAN), 1)
+        spread = one_hot(iota((CHUNKS, group * 2 * SPAN), 0) == index * group + (lanes >> 8))
         target = jnp.dot(back_rows[...], spread, preferred_element_type=F32)
-        table = one_hot(target == iota((CHUNK_ROWS, 2 * SPAN), 1).astype(F32))
-        rows = jnp.concatenate(
-            [
-                mixed[which, pl.ds(pl.multiple_of(firsts[chunk, which], 16), SPAN), :]
-                for which in range(2)
-            ],
-            axis=0,
-        )
-        out_ref[pl.ds(pl.multiple_of(chunk * CHUNK_ROWS, 16), CHUNK_ROWS), :] = jnp.dot(
-            table, rows, preferred_element_type=F32
-        ).astype(BF16)
+        for inner in range(group):
+            chunk = index * group + inner
+            table = one_hot(target[:, inner * 2 * SPAN : (inner + 1) * 2 * SPAN] == columns)
+            rows = jnp.concatenate(
+                [
+                    mixed[which, pl.ds(pl.multiple_of(firsts[chunk, which], 16), SPAN), :]
+                    for which in range(2)
+                ],
+                axis=0,
+            )
+            result[chunk * CHUNK_ROWS : (chunk + 1) * CHUNK_ROWS, :] = jnp.dot(
+                table, rows, preferred_element_type=F32
+            ).astype(BF16)
+        span = pl.ds(index * group * CHUNK_ROWS, group * CHUNK_ROWS)
+        sent.append(pltpu.make_async_copy(result.at[span], out_hbm.at[span], leaving.at[index]))
+        sent[index].start()
+    for copy in sent:
+        copy.wait()
 
 
 def cluster_call(pool):
     return pl.pallas_call(
         cluster_kernel,
         in_specs=[pl.BlockSpec(memory_space=pl.ANY)],
-        out_specs=pl.BlockSpec(memory_space=pltpu.VMEM),
+        out_specs=pl.BlockSpec(memory_space=pl.ANY),
         out_shape=jax.ShapeDtypeStruct((SHARDS * POOL, HD), BF16),
         scratch_shapes=[
             pltpu.VMEM((SHARDS, PACK, HD), BF16),
@@ -379,12 +419,14 @@
             pltpu.VMEM((2, 1, QBLOCK), F32),
             pltpu.VMEM((2, HD, CSIZE), BF16),
             pltpu.VMEM((CHUNKS, SHARDS), jnp.int32),
-            pltpu.VMEM((3, CHUNKS, SHARDS), jnp.int32),
+            pltpu.VMEM((CHUNKS, SHARDS), jnp.int32),
             pltpu.VMEM((CHUNK_ROWS, CHUNKS), BF16),
             pltpu.VMEM((CHUNKS, SHARDS), jnp.int32),
             pltpu.SMEM((CHUNKS, SHARDS), jnp.int32),
             pltpu.SemaphoreType.DMA((PARTS + 1,)),
             pltpu.SemaphoreType.DMA,
+            pltpu.VMEM((SHARDS * POOL, HD), BF16),
+            pltpu.SemaphoreType.DMA((PARTS,)),
         ],
         compiler_params=pltpu.CompilerParams(vmem_limit_bytes=VMEM),
         name="cluster",

time: 133 us -> 131 us (0.985)
  Pallas kernels: 51.9 us -> 49.7 us
    pallas_call x1, Pallas kernels: 23.4 us -> 20.9 us  [cluster_call(): pl.pallas_call(cluster_kernel, in_specs=[pl.BlockSpec(memory_space=pl.ANY...]
  transfers between devices with their start and end apart: 3 -> 3, of which waited for: 2 -> 2; matrix products, arithmetic and copies ran while one was open for 8% -> 8% of each run, Pallas kernels for 26% -> 24%
where the time goes in v5:
time: 131 us
  Pallas kernels  49.7 us (38%)
  waiting for transfers between devices  47.7 us (36%)
  starting transfers between devices  21 us (16%)
  local copies, waits for them, and re-layouts  5.07 us (4%)
  other arithmetic  3.52 us (3%)
  matrix products  3.48 us (3%)
    all_to_all x1, waiting for transfers between devices, body(): lax.all_to_all(placed, AXES, split_axis=0, concat_axis=0, tiled=True)  41.4 us
    pallas_call x1, Pallas kernels, cluster_call(): pl.pallas_call(cluster_kernel, in_specs=[pl.BlockSpec(memory_space=pl.ANY...  20.9 us
    all_to_all x1, starting transfers between devices, body(): lax.all_to_all(placed, AXES, split_axis=0, concat_axis=0, tiled=True)  12 us
    pallas_call x1, Pallas kernels, pre_call(): pl.pallas_call(pre_kernel, in_specs=[pl.BlockSpec(memory_space=pl.ANY), p...  11.2 us
    pallas_call x1, Pallas kernels, window_call(): pl.pallas_call(window_kernel, grid=(1,), in_specs=[pl.BlockSpec(memory_sp...  10.8 us
    pallas_call x1, Pallas kernels, post_call(): pl.pallas_call(post_kernel, in_specs=[pl.BlockSpec(memory_space=pl.ANY),...  6.78 us
    all_to_all x1, waiting for transfers between devices, body(): lax.all_to_all(finished.reshape(SHARDS, POOL, HD), AXES, split_axis=0, co...  6.23 us
    all_to_all x1, starting transfers between devices, body(): lax.all_to_all(finished.reshape(SHARDS, POOL, HD), AXES, split_axis=0, co...  5.32 us
  transfers between devices with their start and end apart: 3, of which 2 were waited for; matrix products, arithmetic and copies ran while one was open for 8% of the time, Pallas kernels for 24%

profile of v5, /device:TPU:1, one launch (start us, length us, event | category | flops | bytes accessed | tf_op | source)
XLA Modules:
  0.0 130.8 jit_solution(13611775181962331305)
XLA Ops:
  0.0 0.0 copy-start
  0.0 11.2 %place.1 = bf16[128,128,128]{2,1,0:T(8,128)(2,1)} custom-call(bf16[512,1024]{1,0:T(8,128)(2,1)} %act_ref.1, f32[1,1024]{1,0:T(1,128)} %bitcast.18, bf16[1024,3072]{1,0:T(8,128)(2,1)} %w_hbm.2, s32[8,512]{1,0:T(8,128)} %bitcast.16), custom_call_target="tpu_custom_call" | custom-call | tf_op jit(solution)/shard_map/place/pallas_call | solution.py:140
  11.2 0.0 copy-start.3
  11.2 12.0 %all-to-all-start = ((bf16[128,128,128]{2,1,0:T(8,128)(2,1)}), bf16[128,128,128]{2,1,0:T(8,128)(2,1)}, u32[]{:S(2)}, u32[]{:S(2)}) async-start(bf16[128,128,128]{2,1,0:T(8,128)(2,1)} %place.1), calls=%async_computation | async-start | bytes 8388608 | tf_op jit(solution)/shard_map/all_to_all | solution.py:501
  23.2 1.5 %fusion = f32[512]{0:T(512)S(1)} fusion(bf16[512,1024]{1,0:T(8,128)(2,1)} %act_ref.1), kind=kLoop, calls=%fused_computation.3 | loop fusion | flops 1572352 | bytes 1050624 | tf_op jit(solution)/shard_map/reduce_sum | solution.py:54
  24.7 3.1 %convolution_convert_fusion.qkv_ref = bf16[512,1536]{1,0:T(8,128)(2,1)S(1)} fusion(bf16[1024,1536]{1,0:T(8,128)(2,1)S(1)} %copy-done, bf16[512,1024]{1,0:T(8,128)(2,1)} %act_ref.1, f32[1024]{0:T(1024)S(1)} %copy-done.3, f32[512]{0:T(512)S(1)} %add_rsqrt_fusion), kind=kOutput, calls=%fused_computation | convolution fusion | flops 1613496320 | bytes 5773312 | tf_op jit(solution)/shard_map/dot_general | solution.py:503
  27.8 1.2 copy-done.1
  29.1 1.1 slice.4
  30.2 3.7 %collective-permute-start = (bf16[512,1024]{1,0:T(8,128)(2,1)}, bf16[512,1024]{1,0:T(8,128)(2,1)}, u32[]{:S(2)}, u32[]{:S(2)}) collective-permute-start(bf16[512,1024]{1,0:T(8,128)(2,1)} %slice.4), channel_id=1, source_target_pairs={{0,1},{1,2},{2,3},{3,4},{4,5},{5,6},{6,7},{7,8},{8,9},{9,10},{10,1... | collective-permute-start | bytes 3145736 | tf_op jit(solution)/shard_map/ppermute | solution.py:509
  33.9 0.1 eq.33
  34.0 0.1 bitcast_compare_fusion
  34.2 0.4 fusion.3
  34.5 41.4 %all-to-all-done.pool_hbm = bf16[128,128,128]{2,1,0:T(8,128)(2,1)} async-done(((bf16[128,128,128]{2,1,0:T(8,128)(2,1)}), bf16[128,128,128]{2,1,0:T(8,128)(2,1)}, u32[]{:S(2)}, u32[]{:S(2)}) %all-to-all-start) | async-done | bytes 4194336 | tf_op jit(solution)/shard_map/all_to_all | solution.py:501
  76.0 20.9 %cluster.1 = bf16[5120,128]{1,0:T(8,128)(2,1)} custom-call(bf16[128,128,128]{2,1,0:T(8,128)(2,1)} %all-to-all-done.pool_hbm), custom_call_target="tpu_custom_call" | custom-call | tf_op jit(solution)/shard_map/cluster/pallas_call | solution.py:408
  96.9 0.0 collective-permute-done.rim_ref
  96.9 5.3 %all-to-all-start.1 = ((bf16[128,40,128]{2,1,0:T(8,128)(2,1)}), bf16[128,40,128]{2,1,0:T(8,128)(2,1)}, u32[]{:S(2)}, u32[]{:S(2)}) async-start(bf16[128,40,128]{2,1,0:T(8,128)(2,1)} %bitcast.15), calls=%async_computation.1 | async-start | bytes 2621440 | tf_op jit(solution)/shard_map/all_to_all | solution.py:512
  102.3 0.1 copy.19
  102.4 0.8 copy.22
  103.3 0.8 copy.20
  104.1 0.8 copy.21
  104.9 1.8 %select_add_fusion.slot_ref = s32[512,8]{1,0:T(8,128)} fusion(s32[512,8]{1,0:T(8,128)} %copy.22, s32[512,8]{1,0:T(8,128)} %copy.20, s32[512,8]{1,0:T(8,128)} %copy.21, s32[512,8]{1,0:T(8,128)S(1)} %copy.19), kind=kLoop, calls=%fused_computation.14 | loop fusion | flops 16384 | bytes 81920 | tf_op jit(solution)/shard_map/add | solution.py:495
  106.8 10.8 %window.1.base_hbm = f32[512,1024]{1,0:T(8,128)} custom-call(s32[1]{0:T(128)} %bitcast.8.first_ref, bf16[512,1536]{1,0:T(8,128)(2,1)} %copy-done.1, bf16[512,1024]{1,0:T(8,128)(2,1)} %collective-permute-done.rim_ref, bf16[512,1024]{1,0:T(8,128)(2,1)} %act_ref.1, bf16[1536,1024]{1,0:T(8,128)(2,1)} %w_hbm.3), custom_call_target="tpu_custom_call" | custom-call | flops 10000000000 | bytes 10000000 | tf_op jit(solution)/shard_map/window/pallas_call | solution.py:200
  117.5 6.2 %all-to-all-done.1 = bf16[128,40,128]{2,1,0:T(8,128)(2,1)} async-done(((bf16[128,40,128]{2,1,0:T(8,128)(2,1)}), bf16[128,40,128]{2,1,0:T(8,128)(2,1)}, u32[]{:S(2)}, u32[]{:S(2)}) %all-to-all-start.1) | async-done | bytes 1310752 | tf_op jit(solution)/shard_map/all_to_all | solution.py:512
  123.8 6.8 %collect.1 = bf16[512,1024]{1,0:T(8,128)(2,1)} custom-call(bf16[5120,128]{1,0:T(8,128)(2,1)} %bitcast.3.back_hbm, s32[512,8]{1,0:T(8,128)} %select_add_fusion.slot_ref, f32[512,1024]{1,0:T(8,128)} %window.1.base_hbm, bf16[1536,1024]{1,0:T(8,128)(2,1)} %w_hbm.3), custom_call_target="tpu_custom_call" | custom-call | tf_op jit(solution)/shard_map/collect/pallas_call | solution.py:465
  (10 shorter events, 0.0 us)
Async XLA Ops:
  0.0 24.7 %copy-start = (bf16[1024,1536]{1,0:T(8,128)(2,1)S(1)}, bf16[1024,1536]{1,0:T(8,128)(2,1)}, u32[]{:S(2)}) copy-start(bf16[1024,1536]{1,0:T(8,128)(2,1)} %param.8) | copy-start | bytes 9437188
  11.2 13.5 %copy-start.3 = (f32[1024]{0:T(1024)S(1)}, f32[1024]{0:T(1024)}, u32[]{:S(2)}) copy-start(f32[1024]{0:T(1024)} %param.7) | copy-start | bytes 12292
  11.2 64.8 %all-to-all-start = ((bf16[128,128,128]{2,1,0:T(8,128)(2,1)}), bf16[128,128,128]{2,1,0:T(8,128)(2,1)}, u32[]{:S(2)}, u32[]{:S(2)}) async-start(bf16[128,128,128]{2,1,0:T(8,128)(2,1)} %place.1), calls=%async_computation | async-start | bytes 8388608 | tf_op jit(solution)/shard_map/all_to_all | solution.py:501
  27.8 1.2 copy-start.1
  29.1 4.9 %copy-start.2 = (s32[512,8]{0,1:T(8,128)S(1)}, s32[512,8]{0,1:T(8,128)}, u32[]{:S(2)}) copy-start(s32[512,8]{0,1:T(8,128)} %param.11) | copy-start | bytes 49156
  30.2 66.7 %collective-permute-start = (bf16[512,1024]{1,0:T(8,128)(2,1)}, bf16[512,1024]{1,0:T(8,128)(2,1)}, u32[]{:S(2)}, u32[]{:S(2)}) collective-permute-start(bf16[512,1024]{1,0:T(8,128)(2,1)} %slice.4), channel_id=1, source_target_pairs={{0,1},{1,2},{2,3},{3,4},{4,5},{5,6},{6,7},{7,8},{8,9},{9,10},{10,1... | collective-permute-start | bytes 3145736 | tf_op jit(solution)/shard_map/ppermute | solution.py:509
  96.9 26.8 %all-to-all-start.1 = ((bf16[128,40,128]{2,1,0:T(8,128)(2,1)}), bf16[128,40,128]{2,1,0:T(8,128)(2,1)}, u32[]{:S(2)}, u32[]{:S(2)}) async-start(bf16[128,40,128]{2,1,0:T(8,128)(2,1)} %bitcast.15), calls=%async_computation.1 | async-start | bytes 2621440 | tf_op jit(solution)/shard_map/all_to_all | solution.py:512

commit v6 on v5

--- a/solution.py
+++ b/solution.py
@@ -433,7 +433,11 @@
     )(pool)
 
 
-def post_kernel(back_hbm, slot_ref, base_hbm, w_hbm, out_ref, back, base, weights, mix, sems):
+def post_kernel(
+    back_hbm, slot_hbm, base_hbm, w_hbm, out_hbm, back, slots, base, weights, mix, out, sems, leaving
+):
+    slot_copy = pltpu.make_async_copy(slot_hbm, slots, sems.at[HC // 2 + 2])
+    slot_copy.start()
     copies = []
     for index in range(HC // 2):
         span = pl.ds(index * 2 * REGION, 2 * REGION)
@@ -445,20 +449,27 @@
     for copy in copies:
         copy.start()
     columns = iota((TOK, REGION), 1)
+    slot_copy.wait()
     for head in range(HC):
         if head % 2 == 0:
             copies[head // 2].wait()
-        table = one_hot(columns == slot_ref[:, head : head + 1])
+        table = one_hot(columns == slots[:, head : head + 1])
         mix[:, head * HD : (head + 1) * HD] = jnp.dot(
             table, back[head * REGION : (head + 1) * REGION, :], preferred_element_type=F32
         ).astype(BF16)
     copies[-2].wait()
     copies[-1].wait()
-    for low in range(0, TOK, 256):
-        rows = slice(low, low + 256)
-        out_ref[rows, :] = (
+    sent = []
+    for index in range(PARTS):
+        rows = slice(index * TOK // PARTS, (index + 1) * TOK // PARTS)
+        out[rows, :] = (
             base[rows, :] + jnp.dot(mix[rows, :], weights[...], preferred_element_type=F32)
         ).astype(BF16)
+        span = pl.ds(index * TOK // PARTS, TOK // PARTS)
+        sent.append(pltpu.make_async_copy(out.at[span], out_hbm.at[span], leaving.at[index]))
+        sent[index].start()
+    for copy in sent:
+        copy.wait()
 
 
 def post_call(back, slot, base, w_output):
@@ -466,18 +477,21 @@
         post_kernel,
         in_specs=[
             pl.BlockSpec(memory_space=pl.ANY),
-            pl.BlockSpec(memory_space=pltpu.VMEM),
+            pl.BlockSpec(memory_space=pl.ANY),
             pl.BlockSpec(memory_space=pl.ANY),
             pl.BlockSpec(memory_space=pl.ANY),
         ],
-        out_specs=pl.BlockSpec(memory_space=pltpu.VMEM),
+        out_specs=pl.BlockSpec(memory_space=pl.ANY),
         out_shape=jax.ShapeDtypeStruct((TOK, D), BF16),
         scratch_shapes=[
             pltpu.VMEM((HC * REGION, HD), BF16),
+            pltpu.VMEM((TOK, HC), jnp.int32),
             pltpu.VMEM((TOK, D), F32),
             pltpu.VMEM((HC * HD, D), BF16),
             pltpu.VMEM((TOK, HC * HD), BF16),
-            pltpu.SemaphoreType.DMA((HC // 2 + 2,)),
+            pltpu.VMEM((TOK, D), BF16),
+            pltpu.SemaphoreType.DMA((HC // 2 + 3,)),
+            pltpu.SemaphoreType.DMA((PARTS,)),
         ],
         compiler_params=pltpu.CompilerParams(vmem_limit_bytes=VMEM),
         name="collect",

time: 131 us -> 130 us (level)
  no operation moved by 1% of the time
where the time goes in v6:
time: 130 us
  Pallas kernels  48.6 us (37%)
  waiting for transfers between devices  47.7 us (37%)
  starting transfers between devices  21 us (16%)
  local copies, waits for them, and re-layouts  5.07 us (4%)
  other arithmetic  3.52 us (3%)
  matrix products  3.48 us (3%)
    all_to_all x1, waiting for transfers between devices, body(): lax.all_to_all(placed, AXES, split_axis=0, concat_axis=0, tiled=True)  41.4 us
    pallas_call x1, Pallas kernels, cluster_call(): pl.pallas_call(cluster_kernel, in_specs=[pl.BlockSpec(memory_space=pl.ANY...  20.9 us
    all_to_all x1, starting transfers between devices, body(): lax.all_to_all(placed, AXES, split_axis=0, concat_axis=0, tiled=True)  12 us
    pallas_call x1, Pallas kernels, pre_call(): pl.pallas_call(pre_kernel, in_specs=[pl.BlockSpec(memory_space=pl.ANY), p...  11.2 us
    pallas_call x1, Pallas kernels, window_call(): pl.pallas_call(window_kernel, grid=(1,), in_specs=[pl.BlockSpec(memory_sp...  10.8 us
    all_to_all x1, waiting for transfers between devices, body(): lax.all_to_all(finished.reshape(SHARDS, POOL, HD), AXES, split_axis=0, co...  6.23 us
    pallas_call x1, Pallas kernels, post_call(): pl.pallas_call(post_kernel, in_specs=[pl.BlockSpec(memory_space=pl.ANY),...  5.7 us
    all_to_all x1, starting transfers between devices, body(): lax.all_to_all(finished.reshape(SHARDS, POOL, HD), AXES, split_axis=0, co...  5.32 us
  transfers between devices with their start and end apart: 3, of which 2 were waited for; matrix products, arithmetic and copies ran while one was open for 8% of the time, Pallas kernels for 24%

profile of v6, /device:TPU:1, one launch (start us, length us, event | category | flops | bytes accessed | tf_op | source)
XLA Modules:
  0.0 129.7 jit_solution(13376759318954078773)
XLA Ops:
  0.0 11.2 %place.1 = bf16[128,128,128]{2,1,0:T(8,128)(2,1)} custom-call(bf16[512,1024]{1,0:T(8,128)(2,1)} %act_ref.1, f32[1,1024]{1,0:T(1,128)} %bitcast.18, bf16[1024,3072]{1,0:T(8,128)(2,1)} %w_hbm.2, s32[8,512]{1,0:T(8,128)} %bitcast.16), custom_call_target="tpu_custom_call" | custom-call | tf_op jit(solution)/shard_map/place/pallas_call | solution.py:140
  11.2 0.0 copy-start.3
  11.2 12.0 %all-to-all-start = ((bf16[128,128,128]{2,1,0:T(8,128)(2,1)}), bf16[128,128,128]{2,1,0:T(8,128)(2,1)}, u32[]{:S(2)}, u32[]{:S(2)}) async-start(bf16[128,128,128]{2,1,0:T(8,128)(2,1)} %place.1), calls=%async_computation | async-start | bytes 8388608 | tf_op jit(solution)/shard_map/all_to_all | solution.py:515
  23.2 1.5 %fusion = f32[512]{0:T(512)S(1)} fusion(bf16[512,1024]{1,0:T(8,128)(2,1)} %act_ref.1), kind=kLoop, calls=%fused_computation.3 | loop fusion | flops 1572352 | bytes 1050624 | tf_op jit(solution)/shard_map/reduce_sum | solution.py:54
  24.7 0.0 copy-done
  24.7 3.1 %convolution_convert_fusion.qkv_ref = bf16[512,1536]{1,0:T(8,128)(2,1)S(1)} fusion(bf16[1024,1536]{1,0:T(8,128)(2,1)S(1)} %copy-done, bf16[512,1024]{1,0:T(8,128)(2,1)} %act_ref.1, f32[1024]{0:T(1024)S(1)} %copy-done.3, f32[512]{0:T(512)S(1)} %add_rsqrt_fusion), kind=kOutput, calls=%fused_computation | convolution fusion | flops 1613496320 | bytes 5773312 | tf_op jit(solution)/shard_map/dot_general | solution.py:517
  27.8 1.2 copy-done.1
  29.1 1.1 slice.4
  30.2 3.7 %collective-permute-start = (bf16[512,1024]{1,0:T(8,128)(2,1)}, bf16[512,1024]{1,0:T(8,128)(2,1)}, u32[]{:S(2)}, u32[]{:S(2)}) collective-permute-start(bf16[512,1024]{1,0:T(8,128)(2,1)} %slice.4), channel_id=1, source_target_pairs={{0,1},{1,2},{2,3},{3,4},{4,5},{5,6},{6,7},{7,8},{8,9},{9,10},{10,1... | collective-permute-start | bytes 3145736 | tf_op jit(solution)/shard_map/ppermute | solution.py:523
  33.9 0.1 eq.33
  34.0 0.1 bitcast_compare_fusion
  34.2 0.4 fusion.3
  34.5 41.4 %all-to-all-done.pool_hbm = bf16[128,128,128]{2,1,0:T(8,128)(2,1)} async-done(((bf16[128,128,128]{2,1,0:T(8,128)(2,1)}), bf16[128,128,128]{2,1,0:T(8,128)(2,1)}, u32[]{:S(2)}, u32[]{:S(2)}) %all-to-all-start) | async-done | bytes 4194336 | tf_op jit(solution)/shard_map/all_to_all | solution.py:515
  76.0 20.9 %cluster.1 = bf16[5120,128]{1,0:T(8,128)(2,1)} custom-call(bf16[128,128,128]{2,1,0:T(8,128)(2,1)} %all-to-all-done.pool_hbm), custom_call_target="tpu_custom_call" | custom-call | tf_op jit(solution)/shard_map/cluster/pallas_call | solution.py:408
  96.9 0.0 collective-permute-done.rim_ref
  96.9 5.3 %all-to-all-start.1 = ((bf16[128,40,128]{2,1,0:T(8,128)(2,1)}), bf16[128,40,128]{2,1,0:T(8,128)(2,1)}, u32[]{:S(2)}, u32[]{:S(2)}) async-start(bf16[128,40,128]{2,1,0:T(8,128)(2,1)} %bitcast.15), calls=%async_computation.1 | async-start | bytes 2621440 | tf_op jit(solution)/shard_map/all_to_all | solution.py:526
  102.3 0.1 copy.19
  102.4 0.8 copy.22
  103.3 0.8 copy.20
  104.1 0.8 copy.21
  104.9 1.8 %select_add_fusion.slot_hbm = s32[512,8]{1,0:T(8,128)} fusion(s32[512,8]{1,0:T(8,128)} %copy.22, s32[512,8]{1,0:T(8,128)} %copy.20, s32[512,8]{1,0:T(8,128)} %copy.21, s32[512,8]{1,0:T(8,128)S(1)} %copy.19), kind=kLoop, calls=%fused_computation.14 | loop fusion | flops 16384 | bytes 81920 | tf_op jit(solution)/shard_map/add | solution.py:509
  106.8 10.8 %window.1.base_hbm = f32[512,1024]{1,0:T(8,128)} custom-call(s32[1]{0:T(128)} %bitcast.8.first_ref, bf16[512,1536]{1,0:T(8,128)(2,1)} %copy-done.1, bf16[512,1024]{1,0:T(8,128)(2,1)} %collective-permute-done.rim_ref, bf16[512,1024]{1,0:T(8,128)(2,1)} %act_ref.1, bf16[1536,1024]{1,0:T(8,128)(2,1)} %w_hbm.3), custom_call_target="tpu_custom_call" | custom-call | flops 10000000000 | bytes 10000000 | tf_op jit(solution)/shard_map/window/pallas_call | solution.py:200
  117.5 6.2 %all-to-all-done.1 = bf16[128,40,128]{2,1,0:T(8,128)(2,1)} async-done(((bf16[128,40,128]{2,1,0:T(8,128)(2,1)}), bf16[128,40,128]{2,1,0:T(8,128)(2,1)}, u32[]{:S(2)}, u32[]{:S(2)}) %all-to-all-start.1) | async-done | bytes 1310752 | tf_op jit(solution)/shard_map/all_to_all | solution.py:526
  123.8 5.7 %collect.1 = bf16[512,1024]{1,0:T(8,128)(2,1)} custom-call(bf16[5120,128]{1,0:T(8,128)(2,1)} %bitcast.3.back_hbm, s32[512,8]{1,0:T(8,128)} %select_add_fusion.slot_hbm, f32[512,1024]{1,0:T(8,128)} %window.1.base_hbm, bf16[1536,1024]{1,0:T(8,128)(2,1)} %w_hbm.3), custom_call_target="tpu_custom_call" | custom-call | tf_op jit(solution)/shard_map/collect/pallas_call | solution.py:476
  (10 shorter events, 0.0 us)
Async XLA Ops:
  0.0 24.7 %copy-start = (bf16[1024,1536]{1,0:T(8,128)(2,1)S(1)}, bf16[1024,1536]{1,0:T(8,128)(2,1)}, u32[]{:S(2)}) copy-start(bf16[1024,1536]{1,0:T(8,128)(2,1)} %param.8) | copy-start | bytes 9437188
  11.2 13.5 %copy-start.3 = (f32[1024]{0:T(1024)S(1)}, f32[1024]{0:T(1024)}, u32[]{:S(2)}) copy-start(f32[1024]{0:T(1024)} %param.7) | copy-start | bytes 12292
  11.2 64.8 %all-to-all-start = ((bf16[128,128,128]{2,1,0:T(8,128)(2,1)}), bf16[128,128,128]{2,1,0:T(8,128)(2,1)}, u32[]{:S(2)}, u32[]{:S(2)}) async-start(bf16[128,128,128]{2,1,0:T(8,128)(2,1)} %place.1), calls=%async_computation | async-start | bytes 8388608 | tf_op jit(solution)/shard_map/all_to_all | solution.py:515
  27.8 1.2 copy-start.1
  29.1 4.9 %copy-start.2 = (s32[512,8]{0,1:T(8,128)S(1)}, s32[512,8]{0,1:T(8,128)}, u32[]{:S(2)}) copy-start(s32[512,8]{0,1:T(8,128)} %param.11) | copy-start | bytes 49156
  30.2 66.7 %collective-permute-start = (bf16[512,1024]{1,0:T(8,128)(2,1)}, bf16[512,1024]{1,0:T(8,128)(2,1)}, u32[]{:S(2)}, u32[]{:S(2)}) collective-permute-start(bf16[512,1024]{1,0:T(8,128)(2,1)} %slice.4), channel_id=1, source_target_pairs={{0,1},{1,2},{2,3},{3,4},{4,5},{5,6},{6,7},{7,8},{8,9},{9,10},{10,1... | collective-permute-start | bytes 3145736 | tf_op jit(solution)/shard_map/ppermute | solution.py:523
  96.9 26.8 %all-to-all-start.1 = ((bf16[128,40,128]{2,1,0:T(8,128)(2,1)}), bf16[128,40,128]{2,1,0:T(8,128)(2,1)}, u32[]{:S(2)}, u32[]{:S(2)}) async-start(bf16[128,40,128]{2,1,0:T(8,128)(2,1)} %bitcast.15), calls=%async_computation.1 | async-start | bytes 2621440 | tf_op jit(solution)/shard_map/all_to_all | solution.py:526

commit v7 on v6

--- a/solution.py
+++ b/solution.py
@@ -127,9 +127,9 @@
                 jnp.dot(pick, size, preferred_element_type=F32).reshape(GROUPS, TAIL, HD)
             )
             stage[groups, 3 * MAIN :, :] = jnp.concatenate(tails, axis=1).astype(BF16)
-        span = pl.ds(step * HEADS_STEP * GROUPS, HEADS_STEP * GROUPS)
-        sent.append(pltpu.make_async_copy(stage.at[span], out_hbm.at[span], leaving.at[step]))
-        sent[step].start()
+            span = pl.ds(head * GROUPS, GROUPS)
+            sent.append(pltpu.make_async_copy(stage.at[span], out_hbm.at[span], leaving.at[head]))
+            sent[head].start()
         qkv = later
     for copy in sent:
         copy.wait()
@@ -155,7 +155,7 @@
             pltpu.VMEM((HC * CLUSTERS, HD), BF16),
             pltpu.VMEM((SHARDS, PACK, HD), BF16),
             pltpu.SemaphoreType.DMA((steps + 1,)),
-            pltpu.SemaphoreType.DMA((steps,)),
+            pltpu.SemaphoreType.DMA((HC,)),
         ],
         compiler_params=pltpu.CompilerParams(vmem_limit_bytes=VMEM),
         name="place",

time: 130 us -> 130 us (level)
  no operation moved by 1% of the time
where the time goes in v7:
time: 130 us
  Pallas kernels  48.4 us (37%)
  waiting for transfers between devices  47.7 us (37%)
  starting transfers between devices  21 us (16%)
  local copies, waits for them, and re-layouts  5.07 us (4%)
  other arithmetic  3.52 us (3%)
  matrix products  3.49 us (3%)
    all_to_all x1, waiting for transfers between devices, body(): lax.all_to_all(placed, AXES, split_axis=0, concat_axis=0, tiled=True)  41.4 us
    pallas_call x1, Pallas kernels, cluster_call(): pl.pallas_call(cluster_kernel, in_specs=[pl.BlockSpec(memory_space=pl.ANY...  20.9 us
    all_to_all x1, starting transfers between devices, body(): lax.all_to_all(placed, AXES, split_axis=0, concat_axis=0, tiled=True)  12 us
    pallas_call x1, Pallas kernels, pre_call(): pl.pallas_call(pre_kernel, in_specs=[pl.BlockSpec(memory_space=pl.ANY), p...  11.1 us
    pallas_call x1, Pallas kernels, window_call(): pl.pallas_call(window_kernel, grid=(1,), in_specs=[pl.BlockSpec(memory_sp...  10.8 us
    all_to_all x1, waiting for transfers between devices, body(): lax.all_to_all(finished.reshape(SHARDS, POOL, HD), AXES, split_axis=0, co...  6.23 us
    pallas_call x1, Pallas kernels, post_call(): pl.pallas_call(post_kernel, in_specs=[pl.BlockSpec(memory_space=pl.ANY),...  5.7 us
    all_to_all x1, starting transfers between devices, body(): lax.all_to_all(finished.reshape(SHARDS, POOL, HD), AXES, split_axis=0, co...  5.33 us
  transfers between devices with their start and end apart: 3, of which 2 were waited for; matrix products, arithmetic and copies ran while one was open for 8% of the time, Pallas kernels for 24%

profile of v7, /device:TPU:1, one launch (start us, length us, event | category | flops | bytes accessed | tf_op | source)
XLA Modules:
  0.0 129.6 jit_solution(636420215934219390)
XLA Ops:
  0.0 0.0 copy-start
  0.0 11.1 %place.1 = bf16[128,128,128]{2,1,0:T(8,128)(2,1)} custom-call(bf16[512,1024]{1,0:T(8,128)(2,1)} %act_ref.1, f32[1,1024]{1,0:T(1,128)} %bitcast.18, bf16[1024,3072]{1,0:T(8,128)(2,1)} %w_hbm.2, s32[8,512]{1,0:T(8,128)} %bitcast.16), custom_call_target="tpu_custom_call" | custom-call | tf_op jit(solution)/shard_map/place/pallas_call | solution.py:140
  11.1 0.0 copy-start.3
  11.1 12.0 %all-to-all-start = ((bf16[128,128,128]{2,1,0:T(8,128)(2,1)}), bf16[128,128,128]{2,1,0:T(8,128)(2,1)}, u32[]{:S(2)}, u32[]{:S(2)}) async-start(bf16[128,128,128]{2,1,0:T(8,128)(2,1)} %place.1), calls=%async_computation | async-start | bytes 8388608 | tf_op jit(solution)/shard_map/all_to_all | solution.py:515
  23.0 1.5 %fusion = f32[512]{0:T(512)S(1)} fusion(bf16[512,1024]{1,0:T(8,128)(2,1)} %act_ref.1), kind=kLoop, calls=%fused_computation.3 | loop fusion | flops 1572352 | bytes 1050624 | tf_op jit(solution)/shard_map/reduce_sum | solution.py:54
  24.6 3.1 %convolution_convert_fusion.qkv_ref = bf16[512,1536]{1,0:T(8,128)(2,1)S(1)} fusion(bf16[1024,1536]{1,0:T(8,128)(2,1)S(1)} %copy-done, bf16[512,1024]{1,0:T(8,128)(2,1)} %act_ref.1, f32[1024]{0:T(1024)S(1)} %copy-done.3, f32[512]{0:T(512)S(1)} %add_rsqrt_fusion), kind=kOutput, calls=%fused_computation | convolution fusion | flops 1613496320 | bytes 5773312 | tf_op jit(solution)/shard_map/dot_general | solution.py:517
  27.7 1.2 copy-done.1
  28.9 1.1 slice.4
  30.1 3.7 %collective-permute-start = (bf16[512,1024]{1,0:T(8,128)(2,1)}, bf16[512,1024]{1,0:T(8,128)(2,1)}, u32[]{:S(2)}, u32[]{:S(2)}) collective-permute-start(bf16[512,1024]{1,0:T(8,128)(2,1)} %slice.4), channel_id=1, source_target_pairs={{0,1},{1,2},{2,3},{3,4},{4,5},{5,6},{6,7},{7,8},{8,9},{9,10},{10,1... | collective-permute-start | bytes 3145736 | tf_op jit(solution)/shard_map/ppermute | solution.py:523
  33.8 0.1 eq.33
  33.9 0.1 bitcast_compare_fusion
  34.0 0.4 fusion.3
  34.4 41.4 %all-to-all-done.pool_hbm = bf16[128,128,128]{2,1,0:T(8,128)(2,1)} async-done(((bf16[128,128,128]{2,1,0:T(8,128)(2,1)}), bf16[128,128,128]{2,1,0:T(8,128)(2,1)}, u32[]{:S(2)}, u32[]{:S(2)}) %all-to-all-start) | async-done | bytes 4194336 | tf_op jit(solution)/shard_map/all_to_all | solution.py:515
  75.9 20.9 %cluster.1 = bf16[5120,128]{1,0:T(8,128)(2,1)} custom-call(bf16[128,128,128]{2,1,0:T(8,128)(2,1)} %all-to-all-done.pool_hbm), custom_call_target="tpu_custom_call" | custom-call | tf_op jit(solution)/shard_map/cluster/pallas_call | solution.py:408
  96.8 0.0 collective-permute-done.rim_ref
  96.8 5.3 %all-to-all-start.1 = ((bf16[128,40,128]{2,1,0:T(8,128)(2,1)}), bf16[128,40,128]{2,1,0:T(8,128)(2,1)}, u32[]{:S(2)}, u32[]{:S(2)}) async-start(bf16[128,40,128]{2,1,0:T(8,128)(2,1)} %bitcast.15), calls=%async_computation.1 | async-start | bytes 2621440 | tf_op jit(solution)/shard_map/all_to_all | solution.py:526
  102.2 0.1 copy.19
  102.3 0.8 copy.22
  103.2 0.8 copy.20
  104.0 0.8 copy.21
  104.8 1.8 %select_add_fusion.slot_hbm = s32[512,8]{1,0:T(8,128)} fusion(s32[512,8]{1,0:T(8,128)} %copy.22, s32[512,8]{1,0:T(8,128)} %copy.20, s32[512,8]{1,0:T(8,128)} %copy.21, s32[512,8]{1,0:T(8,128)S(1)} %copy.19), kind=kLoop, calls=%fused_computation.14 | loop fusion | flops 16384 | bytes 81920 | tf_op jit(solution)/shard_map/add | solution.py:509
  106.7 10.8 %window.1.base_hbm = f32[512,1024]{1,0:T(8,128)} custom-call(s32[1]{0:T(128)} %bitcast.8.first_ref, bf16[512,1536]{1,0:T(8,128)(2,1)} %copy-done.1, bf16[512,1024]{1,0:T(8,128)(2,1)} %collective-permute-done.rim_ref, bf16[512,1024]{1,0:T(8,128)(2,1)} %act_ref.1, bf16[1536,1024]{1,0:T(8,128)(2,1)} %w_hbm.3), custom_call_target="tpu_custom_call" | custom-call | flops 10000000000 | bytes 10000000 | tf_op jit(solution)/shard_map/window/pallas_call | solution.py:200
  117.4 6.2 %all-to-all-done.1 = bf16[128,40,128]{2,1,0:T(8,128)(2,1)} async-done(((bf16[128,40,128]{2,1,0:T(8,128)(2,1)}), bf16[128,40,128]{2,1,0:T(8,128)(2,1)}, u32[]{:S(2)}, u32[]{:S(2)}) %all-to-all-start.1) | async-done | bytes 1310752 | tf_op jit(solution)/shard_map/all_to_all | solution.py:526
  123.7 5.7 %collect.1 = bf16[512,1024]{1,0:T(8,128)(2,1)} custom-call(bf16[5120,128]{1,0:T(8,128)(2,1)} %bitcast.3.back_hbm, s32[512,8]{1,0:T(8,128)} %select_add_fusion.slot_hbm, f32[512,1024]{1,0:T(8,128)} %window.1.base_hbm, bf16[1536,1024]{1,0:T(8,128)(2,1)} %w_hbm.3), custom_call_target="tpu_custom_call" | custom-call | tf_op jit(solution)/shard_map/collect/pallas_call | solution.py:476
  (10 shorter events, 0.0 us)
Async XLA Ops:
  0.0 24.6 %copy-start = (bf16[1024,1536]{1,0:T(8,128)(2,1)S(1)}, bf16[1024,1536]{1,0:T(8,128)(2,1)}, u32[]{:S(2)}) copy-start(bf16[1024,1536]{1,0:T(8,128)(2,1)} %param.8) | copy-start | bytes 9437188
  11.1 13.5 %copy-start.3 = (f32[1024]{0:T(1024)S(1)}, f32[1024]{0:T(1024)}, u32[]{:S(2)}) copy-start(f32[1024]{0:T(1024)} %param.7) | copy-start | bytes 12292
  11.1 64.8 %all-to-all-start = ((bf16[128,128,128]{2,1,0:T(8,128)(2,1)}), bf16[128,128,128]{2,1,0:T(8,128)(2,1)}, u32[]{:S(2)}, u32[]{:S(2)}) async-start(bf16[128,128,128]{2,1,0:T(8,128)(2,1)} %place.1), calls=%async_computation | async-start | bytes 8388608 | tf_op jit(solution)/shard_map/all_to_all | solution.py:515
  27.7 1.2 copy-start.1
  28.9 4.9 %copy-start.2 = (s32[512,8]{0,1:T(8,128)S(1)}, s32[512,8]{0,1:T(8,128)}, u32[]{:S(2)}) copy-start(s32[512,8]{0,1:T(8,128)} %param.11) | copy-start | bytes 49156
  30.1 66.7 %collective-permute-start = (bf16[512,1024]{1,0:T(8,128)(2,1)}, bf16[512,1024]{1,0:T(8,128)(2,1)}, u32[]{:S(2)}, u32[]{:S(2)}) collective-permute-start(bf16[512,1024]{1,0:T(8,128)(2,1)} %slice.4), channel_id=1, source_target_pairs={{0,1},{1,2},{2,3},{3,4},{4,5},{5,6},{6,7},{7,8},{8,9},{9,10},{10,1... | collective-permute-start | bytes 3145736 | tf_op jit(solution)/shard_map/ppermute | solution.py:523
  96.8 26.8 %all-to-all-start.1 = ((bf16[128,40,128]{2,1,0:T(8,128)(2,1)}), bf16[128,40,128]{2,1,0:T(8,128)(2,1)}, u32[]{:S(2)}, u32[]{:S(2)}) async-start(bf16[128,40,128]{2,1,0:T(8,128)(2,1)} %bitcast.15), calls=%async_computation.1 | async-start | bytes 2621440 | tf_op jit(solution)/shard_map/all_to_all | solution.py:526

commit v8 on v6

--- a/solution.py
+++ b/solution.py
@@ -24,7 +24,7 @@
 MAIN = 32
 TAIL = POOL - MAIN
 PACK = 3 * MAIN + 4 * TAIL
-HEADS_STEP = 2
+HEADS_STEP = 4
 CHUNK = 4
 CHUNKS = SHARDS // CHUNK
 CHUNK_ROWS = CHUNK * POOL

time: 130 us -> 130 us (level)
  no operation moved by 1% of the time
where the time goes in v8:
time: 130 us
  Pallas kernels  48.4 us (37%)
  waiting for transfers between devices  47.7 us (37%)
  starting transfers between devices  21 us (16%)
  local copies, waits for them, and re-layouts  5.07 us (4%)
  other arithmetic  3.52 us (3%)
  matrix products  3.48 us (3%)
    all_to_all x1, waiting for transfers between devices, body(): lax.all_to_all(placed, AXES, split_axis=0, concat_axis=0, tiled=True)  41.4 us
    pallas_call x1, Pallas kernels, cluster_call(): pl.pallas_call(cluster_kernel, in_specs=[pl.BlockSpec(memory_space=pl.ANY...  20.9 us
    all_to_all x1, starting transfers between devices, body(): lax.all_to_all(placed, AXES, split_axis=0, concat_axis=0, tiled=True)  12 us
    pallas_call x1, Pallas kernels, pre_call(): pl.pallas_call(pre_kernel, in_specs=[pl.BlockSpec(memory_space=pl.ANY), p...  11 us
    pallas_call x1, Pallas kernels, window_call(): pl.pallas_call(window_kernel, grid=(1,), in_specs=[pl.BlockSpec(memory_sp...  10.8 us
    all_to_all x1, waiting for transfers between devices, body(): lax.all_to_all(finished.reshape(SHARDS, POOL, HD), AXES, split_axis=0, co...  6.24 us
    pallas_call x1, Pallas kernels, post_call(): pl.pallas_call(post_kernel, in_specs=[pl.BlockSpec(memory_space=pl.ANY),...  5.7 us
    all_to_all x1, starting transfers between devices, body(): lax.all_to_all(finished.reshape(SHARDS, POOL, HD), AXES, split_axis=0, co...  5.32 us
  transfers between devices with their start and end apart: 3, of which 2 were waited for; matrix products, arithmetic and copies ran while one was open for 8% of the time, Pallas kernels for 24%

profile of v8, /device:TPU:1, one launch (start us, length us, event | category | flops | bytes accessed | tf_op | source)
XLA Modules:
  0.0 129.5 jit_solution(6848037535037154125)
XLA Ops:
  0.0 0.0 copy-start
  0.0 11.0 %place.1 = bf16[128,128,128]{2,1,0:T(8,128)(2,1)} custom-call(bf16[512,1024]{1,0:T(8,128)(2,1)} %act_ref.1, f32[1,1024]{1,0:T(1,128)} %bitcast.18, bf16[1024,3072]{1,0:T(8,128)(2,1)} %w_hbm.2, s32[8,512]{1,0:T(8,128)} %bitcast.16), custom_call_target="tpu_custom_call" | custom-call | tf_op jit(solution)/shard_map/place/pallas_call | solution.py:140
  11.0 0.0 copy-start.3
  11.1 12.0 %all-to-all-start = ((bf16[128,128,128]{2,1,0:T(8,128)(2,1)}), bf16[128,128,128]{2,1,0:T(8,128)(2,1)}, u32[]{:S(2)}, u32[]{:S(2)}) async-start(bf16[128,128,128]{2,1,0:T(8,128)(2,1)} %place.1), calls=%async_computation | async-start | bytes 8388608 | tf_op jit(solution)/shard_map/all_to_all | solution.py:515
  23.0 1.5 %fusion = f32[512]{0:T(512)S(1)} fusion(bf16[512,1024]{1,0:T(8,128)(2,1)} %act_ref.1), kind=kLoop, calls=%fused_computation.3 | loop fusion | flops 1572352 | bytes 1050624 | tf_op jit(solution)/shard_map/reduce_sum | solution.py:54
  24.6 3.1 %convolution_convert_fusion.qkv_ref = bf16[512,1536]{1,0:T(8,128)(2,1)S(1)} fusion(bf16[1024,1536]{1,0:T(8,128)(2,1)S(1)} %copy-done, bf16[512,1024]{1,0:T(8,128)(2,1)} %act_ref.1, f32[1024]{0:T(1024)S(1)} %copy-done.3, f32[512]{0:T(512)S(1)} %add_rsqrt_fusion), kind=kOutput, calls=%fused_computation | convolution fusion | flops 1613496320 | bytes 5773312 | tf_op jit(solution)/shard_map/dot_general | solution.py:517
  27.7 1.2 copy-done.1
  28.9 1.1 slice.4
  30.0 3.7 %collective-permute-start = (bf16[512,1024]{1,0:T(8,128)(2,1)}, bf16[512,1024]{1,0:T(8,128)(2,1)}, u32[]{:S(2)}, u32[]{:S(2)}) collective-permute-start(bf16[512,1024]{1,0:T(8,128)(2,1)} %slice.4), channel_id=1, source_target_pairs={{0,1},{1,2},{2,3},{3,4},{4,5},{5,6},{6,7},{7,8},{8,9},{9,10},{10,1... | collective-permute-start | bytes 3145736 | tf_op jit(solution)/shard_map/ppermute | solution.py:523
  33.8 0.1 eq.33
  33.9 0.1 bitcast_compare_fusion
  34.0 0.4 fusion.3
  34.4 41.4 %all-to-all-done.pool_hbm = bf16[128,128,128]{2,1,0:T(8,128)(2,1)} async-done(((bf16[128,128,128]{2,1,0:T(8,128)(2,1)}), bf16[128,128,128]{2,1,0:T(8,128)(2,1)}, u32[]{:S(2)}, u32[]{:S(2)}) %all-to-all-start) | async-done | bytes 4194336 | tf_op jit(solution)/shard_map/all_to_all | solution.py:515
  75.8 20.9 %cluster.1 = bf16[5120,128]{1,0:T(8,128)(2,1)} custom-call(bf16[128,128,128]{2,1,0:T(8,128)(2,1)} %all-to-all-done.pool_hbm), custom_call_target="tpu_custom_call" | custom-call | tf_op jit(solution)/shard_map/cluster/pallas_call | solution.py:408
  96.8 0.0 collective-permute-done.rim_ref
  96.8 5.3 %all-to-all-start.1 = ((bf16[128,40,128]{2,1,0:T(8,128)(2,1)}), bf16[128,40,128]{2,1,0:T(8,128)(2,1)}, u32[]{:S(2)}, u32[]{:S(2)}) async-start(bf16[128,40,128]{2,1,0:T(8,128)(2,1)} %bitcast.15), calls=%async_computation.1 | async-start | bytes 2621440 | tf_op jit(solution)/shard_map/all_to_all | solution.py:526
  102.1 0.1 copy.19
  102.3 0.8 copy.22
  103.1 0.8 copy.20
  103.9 0.8 copy.21
  104.8 1.8 %select_add_fusion.slot_hbm = s32[512,8]{1,0:T(8,128)} fusion(s32[512,8]{1,0:T(8,128)} %copy.22, s32[512,8]{1,0:T(8,128)} %copy.20, s32[512,8]{1,0:T(8,128)} %copy.21, s32[512,8]{1,0:T(8,128)S(1)} %copy.19), kind=kLoop, calls=%fused_computation.14 | loop fusion | flops 16384 | bytes 81920 | tf_op jit(solution)/shard_map/add | solution.py:509
  106.6 10.8 %window.1.base_hbm = f32[512,1024]{1,0:T(8,128)} custom-call(s32[1]{0:T(128)} %bitcast.8.first_ref, bf16[512,1536]{1,0:T(8,128)(2,1)} %copy-done.1, bf16[512,1024]{1,0:T(8,128)(2,1)} %collective-permute-done.rim_ref, bf16[512,1024]{1,0:T(8,128)(2,1)} %act_ref.1, bf16[1536,1024]{1,0:T(8,128)(2,1)} %w_hbm.3), custom_call_target="tpu_custom_call" | custom-call | flops 10000000000 | bytes 10000000 | tf_op jit(solution)/shard_map/window/pallas_call | solution.py:200
  117.4 6.2 %all-to-all-done.1 = bf16[128,40,128]{2,1,0:T(8,128)(2,1)} async-done(((bf16[128,40,128]{2,1,0:T(8,128)(2,1)}), bf16[128,40,128]{2,1,0:T(8,128)(2,1)}, u32[]{:S(2)}, u32[]{:S(2)}) %all-to-all-start.1) | async-done | bytes 1310752 | tf_op jit(solution)/shard_map/all_to_all | solution.py:526
  123.6 5.7 %collect.1 = bf16[512,1024]{1,0:T(8,128)(2,1)} custom-call(bf16[5120,128]{1,0:T(8,128)(2,1)} %bitcast.3.back_hbm, s32[512,8]{1,0:T(8,128)} %select_add_fusion.slot_hbm, f32[512,1024]{1,0:T(8,128)} %window.1.base_hbm, bf16[1536,1024]{1,0:T(8,128)(2,1)} %w_hbm.3), custom_call_target="tpu_custom_call" | custom-call | tf_op jit(solution)/shard_map/collect/pallas_call | solution.py:476
  (10 shorter events, 0.0 us)
Async XLA Ops:
  0.0 24.5 %copy-start = (bf16[1024,1536]{1,0:T(8,128)(2,1)S(1)}, bf16[1024,1536]{1,0:T(8,128)(2,1)}, u32[]{:S(2)}) copy-start(bf16[1024,1536]{1,0:T(8,128)(2,1)} %param.8) | copy-start | bytes 9437188
  11.0 13.5 %copy-start.3 = (f32[1024]{0:T(1024)S(1)}, f32[1024]{0:T(1024)}, u32[]{:S(2)}) copy-start(f32[1024]{0:T(1024)} %param.7) | copy-start | bytes 12292
  11.1 64.8 %all-to-all-start = ((bf16[128,128,128]{2,1,0:T(8,128)(2,1)}), bf16[128,128,128]{2,1,0:T(8,128)(2,1)}, u32[]{:S(2)}, u32[]{:S(2)}) async-start(bf16[128,128,128]{2,1,0:T(8,128)(2,1)} %place.1), calls=%async_computation | async-start | bytes 8388608 | tf_op jit(solution)/shard_map/all_to_all | solution.py:515
  27.7 1.2 copy-start.1
  28.9 4.9 %copy-start.2 = (s32[512,8]{0,1:T(8,128)S(1)}, s32[512,8]{0,1:T(8,128)}, u32[]{:S(2)}) copy-start(s32[512,8]{0,1:T(8,128)} %param.11) | copy-start | bytes 49156
  30.0 66.7 %collective-permute-start = (bf16[512,1024]{1,0:T(8,128)(2,1)}, bf16[512,1024]{1,0:T(8,128)(2,1)}, u32[]{:S(2)}, u32[]{:S(2)}) collective-permute-start(bf16[512,1024]{1,0:T(8,128)(2,1)} %slice.4), channel_id=1, source_target_pairs={{0,1},{1,2},{2,3},{3,4},{4,5},{5,6},{6,7},{7,8},{8,9},{9,10},{10,1... | collective-permute-start | bytes 3145736 | tf_op jit(solution)/shard_map/ppermute | solution.py:523
  96.8 26.8 %all-to-all-start.1 = ((bf16[128,40,128]{2,1,0:T(8,128)(2,1)}), bf16[128,40,128]{2,1,0:T(8,128)(2,1)}, u32[]{:S(2)}, u32[]{:S(2)}) async-start(bf16[128,40,128]{2,1,0:T(8,128)(2,1)} %bitcast.15), calls=%async_computation.1 | async-start | bytes 2621440 | tf_op jit(solution)/shard_map/all_to_all | solution.py:526
